TPU v7x, 32 devices: a whole 2x2x4 slice. The times are simulated.
32 devices in a mesh: grp: 2 (over y), ch: 4 (over z), tm: 2 (over x), sub: 2 (over core).
Axes of the slice: x: 2, y: 2, z: 4, core: 2. Of those that a mesh axis runs over, the one named last changes fastest.
Arguments:
- record: bfloat16 [256, 1024], P(('grp', 'ch'), ('tm', 'sub')), parts along dimension 0, may hold values from -8 to 8
- freq_bins: int32 [64], P('grp'), parts along dimension 0, may hold values from 1 to 511, as said below
- wave_limit: int32 [64], P('grp'), parts along dimension 0, may hold values from 1 to 64
- pick_index: int32 [128], P(('grp', 'ch')), parts along dimension 0, may hold values from 0 to 1023
- weight_first: bfloat16 [9, 32], replicated, may hold values from -2 to 2
- weight_second: bfloat16 [9, 32, 32], replicated, may hold values from -0.375 to 0.375
- weight_stride: bfloat16 [4, 64, 32], replicated, may hold values from -0.5 to 0.5
- weight_third: bfloat16 [9, 64, 64], replicated, may hold values from -0.25 to 0.25
- weight_head: bfloat16 [64], replicated, may hold values from -0.75 to 0.75
Outputs:
- filtered: bfloat16 [256, 1024], P(('grp', 'ch'), ('tm', 'sub')), parts along dimension 0
- logits: float32 [128, 512], P(('grp', 'ch'), ('tm', 'sub')), parts along dimension 0
- filtered_grad: float32 [256, 1024], P(('grp', 'ch'), ('tm', 'sub')), parts along dimension 0
There are 2 independent parts, one for each index of `grp`. A program takes and returns all parts, laid end to end along the dimension named above; an argument that names none is the same for every part. Nothing has to cross between parts.
Inputs may be any that keep to these rules, and one draw needn't show every extreme that they name: `freq_bins`: distinct bins, none of them 0 or 512.
All inputs are finite; a program needn't handle non-finite values.
Results may differ from a plain program's by a relative error of at most 0.02.
Values may be sent and summed in bfloat16 or wider, within the bound.
A program may use at most 64 MiB of HBM per device.

v0:
```python
import math

import jax
import jax.numpy as jnp
from jax import lax
from jax.sharding import PartitionSpec as P

SIGMA = 64


def with_halo(block, sides, width):
    for axis, dim in sides:
        count = lax.axis_size(axis)
        forward = [(i, i + 1) for i in range(count - 1)]
        backward = [(target, source) for source, target in forward]
        low = lax.ppermute(
            lax.slice_in_dim(block, block.shape[dim] - width, None, axis=dim), axis, forward
        )
        high = lax.ppermute(lax.slice_in_dim(block, 0, width, axis=dim), axis, backward)
        block = jnp.concatenate([low, block, high], axis=dim)
    return block


def silu_slope(preact):
    sigma_part = jax.nn.sigmoid(preact)
    return sigma_part * (1.0 + preact * (1.0 - sigma_part))


def silu_round(preact):
    return (preact * jax.nn.sigmoid(preact)).astype(jnp.bfloat16)


def conv_forward(padded, weight, height, breadth):
    summed_up = jnp.zeros((weight.shape[1], height, breadth), jnp.float32)
    for kernel_tap in range(9):
        shift_row, shift_col = (kernel_tap // 3, kernel_tap % 3)
        window = padded[:, shift_row : shift_row + height, shift_col : shift_col + breadth]
        summed_up = summed_up + jnp.einsum(
            "oi,ihw->ohw", weight[kernel_tap], window, preferred_element_type=jnp.float32
        )
    return summed_up


def conv_backward(padded_grad, weight, height, breadth):
    summed_up = jnp.zeros((weight.shape[2], height, breadth), jnp.float32)
    for kernel_tap in range(9):
        shift_row, shift_col = (kernel_tap // 3, kernel_tap % 3)
        window = padded_grad[
            :, 2 - shift_row : 2 - shift_row + height, 2 - shift_col : 2 - shift_col + breadth
        ]
        summed_up = summed_up + jnp.einsum(
            "oi,ohw->ihw", weight[kernel_tap], window, preferred_element_type=jnp.float32
        )
    return summed_up


def phase_table(bin_slice, time_index, samples):
    turn_count = bin_slice[:, None] * time_index[None, :] % samples
    phase_angle = turn_count.astype(jnp.float32) * (2.0 * math.pi / samples)
    return (jnp.cos(phase_angle), jnp.sin(phase_angle))


def fourier_tables(length, direction):
    position = jnp.arange(length, dtype=jnp.int32)
    turn_count = position[:, None] * position[None, :] % length
    phase_angle = turn_count.astype(jnp.float32) * (2.0 * math.pi / length)
    cosine = jnp.cos(phase_angle)
    sine_table = jnp.sin(phase_angle) * direction
    upper_half = jnp.stack([cosine, sine_table], axis=1)
    bottom = jnp.stack([-sine_table, cosine], axis=1)
    return jnp.stack([upper_half, bottom], axis=0)


def twiddle_apply(spectra, chan_groups, local_chans, direction):
    total_chans = chan_groups * local_chans
    outer_index = jnp.arange(chan_groups, dtype=jnp.int32)
    inner_index = jnp.arange(local_chans, dtype=jnp.int32)
    turn_count = outer_index[:, None] * inner_index[None, :] % total_chans
    phase_angle = turn_count.astype(jnp.float32) * (2.0 * math.pi / total_chans)
    cosine = jnp.cos(phase_angle)
    sine_table = jnp.sin(phase_angle) * direction
    real_part = spectra[:, 0]
    imag_part = spectra[:, 1]
    new_real = real_part * cosine + imag_part * sine_table
    new_imag = imag_part * cosine - real_part * sine_table
    return jnp.stack([new_real, new_imag], axis=1)


def filter_bins(spectra, limits, chan_groups, local_chans):
    precise = lax.Precision.HIGHEST
    total_chans = chan_groups * local_chans
    sectioned = jnp.einsum(
        "pkqa,fqab->fpkb", fourier_tables(chan_groups, 1.0), spectra, precision=precise
    )
    sectioned = twiddle_apply(sectioned, chan_groups, local_chans, 1.0)
    wave_spec = jnp.einsum(
        "pkqb,fqab->fpak", fourier_tables(local_chans, 1.0), sectioned, precision=precise
    )
    wave_index = (
        jnp.arange(chan_groups, dtype=jnp.int32)[:, None]
        + chan_groups * jnp.arange(local_chans, dtype=jnp.int32)[None, :]
    )
    wave_abs = jnp.minimum(wave_index, total_chans - wave_index)
    passing = (wave_abs[None] <= limits[:, None, None]).astype(jnp.float32)
    wave_spec = wave_spec * passing[:, None]
    sectioned = jnp.einsum(
        "pkqb,fqab->fpak", fourier_tables(local_chans, -1.0), wave_spec, precision=precise
    )
    sectioned = twiddle_apply(sectioned, chan_groups, local_chans, -1.0)
    result = jnp.einsum(
        "pkqa,fqab->fpkb", fourier_tables(chan_groups, -1.0), sectioned, precision=precise
    )
    return result * (1.0 / total_chans)


def local(
    record,
    freq_bins,
    wave_limit,
    pick_index,
    weight_first,
    weight_second,
    weight_stride,
    weight_third,
    weight_head,
):
    precise = lax.Precision.HIGHEST
    local_chans, local_times = record.shape
    chan_groups = lax.axis_size("ch")
    time_groups = lax.axis_size(("tm", "sub"))
    samples = local_times * time_groups
    freq_count = freq_bins.shape[0]
    bins_local = freq_count // (chan_groups * time_groups)
    time_index = lax.axis_index(("tm", "sub")) * local_times + jnp.arange(
        local_times, dtype=jnp.int32
    )
    signal = record.astype(jnp.float32)
    bin_slice = freq_bins
    cosine, sine_table = phase_table(bin_slice, time_index, samples)
    real_part = jnp.einsum("ft,ct->fc", cosine, signal, precision=precise)
    imag_part = -jnp.einsum("ft,ct->fc", sine_table, signal, precision=precise)
    summed = lax.psum_scatter(
        jnp.concatenate([real_part, imag_part], axis=1),
        ("tm", "sub"),
        scatter_dimension=0,
        tiled=True,
    )
    spectrum = summed.astype(jnp.bfloat16)
    gathered = lax.all_to_all(spectrum, "ch", split_axis=0, concat_axis=1, tiled=True)
    freq_block = lax.axis_index(("tm", "sub")) * chan_groups + lax.axis_index("ch")
    arranged = (
        gathered.reshape(bins_local, chan_groups, 2, local_chans)
        .transpose(0, 2, 1, 3)
        .astype(jnp.float32)
    )
    limits = lax.dynamic_slice_in_dim(wave_limit, freq_block * bins_local, bins_local)
    passed = filter_bins(arranged, limits, chan_groups, local_chans).astype(jnp.bfloat16)
    outgoing = passed.transpose(0, 2, 1, 3).reshape(bins_local, chan_groups * 2 * local_chans)
    returned = lax.all_to_all(outgoing, "ch", split_axis=1, concat_axis=0, tiled=True)
    bin_slice = freq_bins
    cosine, sine_table = phase_table(bin_slice, time_index, samples)
    values = lax.all_gather(returned, ("tm", "sub"), axis=0, tiled=True).astype(jnp.float32)
    running = jnp.einsum("fc,ft->ct", values[:, :local_chans], cosine, precision=precise)
    summed_time = running - jnp.einsum(
        "fc,ft->ct", values[:, local_chans:], sine_table, precision=precise
    )
    filtered = (summed_time * (2.0 / samples)).astype(jnp.bfloat16)
    half_chans = local_chans // 2
    half_times = local_times // 2
    weight_first_full = weight_first[:, :, None]
    padded_input = with_halo(filtered[None], (("ch", 1), (("tm", "sub"), 2)), 1)
    pre_first = conv_forward(padded_input, weight_first_full, local_chans, local_times)
    act_first = silu_round(pre_first)
    padded_first = with_halo(act_first, (("ch", 1), (("tm", "sub"), 2)), 1)
    pre_second = conv_forward(padded_first, weight_second, local_chans, local_times)
    act_second = silu_round(pre_second)
    pre_stride = jnp.zeros((weight_stride.shape[1], half_chans, half_times), jnp.float32)
    for kernel_tap in range(4):
        shift_row, shift_col = (kernel_tap // 2, kernel_tap % 2)
        window = act_second[:, shift_row::2, shift_col::2]
        pre_stride = pre_stride + jnp.einsum(
            "oi,ihw->ohw", weight_stride[kernel_tap], window, preferred_element_type=jnp.float32
        )
    act_stride = silu_round(pre_stride)
    padded_stride = with_halo(act_stride, (("ch", 1), (("tm", "sub"), 2)), 1)
    pre_third = conv_forward(padded_stride, weight_third, half_chans, half_times)
    act_third = silu_round(pre_third)
    act_wide = act_third.astype(jnp.float32)
    head_wide = weight_head.astype(jnp.float32)
    logits = jnp.einsum("o,ohw->hw", head_wide, act_wide)
    coarse_index = lax.axis_index(("tm", "sub")) * half_times + jnp.arange(
        half_times, dtype=jnp.int32
    )
    coarse_time = 2.0 * coarse_index.astype(jnp.float32)
    offsets = (coarse_time[None, :] - pick_index[:, None].astype(jnp.float32)) / SIGMA
    target = jnp.exp(-0.5 * offsets * offsets)
    slope_out = jax.nn.sigmoid(logits) - target
    delta_third = (head_wide[:, None, None] * slope_out[None] * silu_slope(pre_third)).astype(
        jnp.bfloat16
    )
    padded_third = with_halo(delta_third, (("ch", 1), (("tm", "sub"), 2)), 1)
    back_stride = conv_backward(padded_third, weight_third, half_chans, half_times)
    delta_stride = (back_stride * silu_slope(pre_stride)).astype(jnp.bfloat16)
    pieces = []
    for kernel_tap in range(4):
        pieces.append(
            jnp.einsum(
                "oi,ohw->ihw",
                weight_stride[kernel_tap],
                delta_stride,
                preferred_element_type=jnp.float32,
            )
        )
    regrid = jnp.stack(
        [jnp.stack([pieces[0], pieces[1]], axis=-1), jnp.stack([pieces[2], pieces[3]], axis=-1)],
        axis=2,
    )
    back_second = regrid.reshape(weight_stride.shape[2], local_chans, local_times)
    delta_second = (back_second * silu_slope(pre_second)).astype(jnp.bfloat16)
    padded_second = with_halo(delta_second, (("ch", 1), (("tm", "sub"), 2)), 1)
    back_first = conv_backward(padded_second, weight_second, local_chans, local_times)
    delta_first = (back_first * silu_slope(pre_first)).astype(jnp.bfloat16)
    padded_delta = with_halo(delta_first, (("ch", 1), (("tm", "sub"), 2)), 1)
    filtered_grad = conv_backward(padded_delta, weight_first_full, local_chans, local_times)[0]
    return (filtered, logits, filtered_grad)


def solution(mesh):
    return jax.shard_map(
        local,
        mesh=mesh,
        in_specs=(
            P(("grp", "ch"), ("tm", "sub")),
            P("grp"),
            P("grp"),
            P(("grp", "ch")),
            P(),
            P(),
            P(),
            P(),
            P(),
        ),
        out_specs=(
            P(("grp", "ch"), ("tm", "sub")),
            P(("grp", "ch"), ("tm", "sub")),
            P(("grp", "ch"), ("tm", "sub")),
        ),
        check_vma=False,
    )
```

profile of v0, /device:TPU:26, one launch (start us, length us, event | category | flops | bytes accessed | tf_op | source)
XLA Modules:
  0.0 198.3 jit_solution(12475618036082609772)
XLA Ops:
  3.4 10.2 %all-reduce = bf16[32,64]{1,0:T(8,128)(2,1)S(1)} all-reduce(f32[32,64]{1,0:T(8,128)S(1)} %pad_maximum_fusion.27), channel_id=2, replica_groups=mesh['grp'=2,'ch'=4,'tm'=2,'sub'=2] {'tm','sub'}, use_global_device_ids=true, to_apply=%region_0.1.clone | all-reduce | flops 2048 | bytes 12288
  16.1 5.1 %all-to-all-start = ((bf16[4,2,64]{2,1,0:T(2,128)(2,1)}), bf16[4,2,64]{2,1,0:T(2,128)(2,1)S(1)}, u32[]{:S(2)}, u32[]{:S(2)}) async-start(bf16[4,2,64]{2,1,0:T(2,128)(2,1)} %bitcast), calls=%async_computation | async-start | bytes 4096 | tf_op jit(solution)/shard_map/all_to_all | solution.py:149
  25.2 6.5 %all-to-all-start.1 = ((bf16[2,4,64]{2,0,1:T(2,128)(2,1)}), bf16[2,4,64]{2,0,1:T(2,128)(2,1)S(1)}, u32[]{:S(2)}, u32[]{:S(2)}) async-start(bf16[2,4,64]{2,0,1:T(2,128)(2,1)} %reshape.529), calls=%async_computation.1 | async-start | bytes 4096 | tf_op jit(solution)/shard_map/all_to_all | solution.py:159
  33.8 5.2 %all_gather.3 = bf16[32,64]{1,0:T(8,128)(2,1)S(1)} all-gather(bf16[8,64]{1,0:T(8,128)(2,1)S(1)} %bitcast.473), channel_id=1, replica_groups=mesh['grp'=2,'ch'=4,'tm'=2,'sub'=2] {'tm','sub'}, dimensions={0}, use_global_device_ids=true | all-gather | bytes 5120 | tf_op jit(solution)/shard_map/all_gather | solution.py:162
  41.0 1.3 collective-permute-start
  42.3 4.5 %collective-permute-start.1 = (bf16[1,1,256]{2,1,0:T(2,128)(2,1)S(1)}, bf16[1,1,256]{2,1,0:T(2,128)(2,1)S(1)}, u32[]{:S(2)}, u32[]{:S(2)}) collective-permute-start(bf16[1,1,256]{2,1,0:T(2,128)(2,1)S(1)} %get-tuple-element.46), channel_id=1, source_target_pairs={{4,0},{8,4},{12,8},{5,1},{9,5},{13,9},{6,2},{10,6},{14,10},{7,3},{... | collective-permute-start | bytes 1544 | tf_op jit(solution)/shard_map/ppermute | solution.py:19
  48.3 1.9 collective-permute-start.2
  50.2 3.6 %collective-permute-start.3 = (bf16[1,34,1]{2,1,0:T(8,128)(2,1)S(1)}, bf16[1,34,1]{2,1,0:T(8,128)(2,1)S(1)}, u32[]{:S(2)}, u32[]{:S(2)}) collective-permute-start(bf16[1,34,1]{2,1,0:T(8,128)(2,1)S(1)} %get-tuple-element.40), channel_id=1, source_target_pairs={{1,0},{2,1},{3,2},{5,4},{6,5},{7,6},{9,8},{10,9},{11,10},{13,12},{... | collective-permute-start | bytes 212 | tf_op jit(solution)/shard_map/ppermute | solution.py:19
  53.9 1.3 collective-permute-done.3
  56.4 1.3 collective-permute-start.4
  57.7 4.7 %collective-permute-start.5 = (bf16[32,1,256]{2,0,1:T(8,128)(2,1)S(1)}, bf16[32,1,256]{2,0,1:T(8,128)(2,1)S(1)}, u32[]{:S(2)}, u32[]{:S(2)}) collective-permute-start(bf16[32,1,256]{2,0,1:T(8,128)(2,1)S(1)} %get-tuple-element.20), channel_id=1, source_target_pairs={{4,0},{8,4},{12,8},{5,1},{9,5},{13,9},{6,2},{10,6},{14,10},{7,3},{... | collective-permute-start | bytes 49160 | tf_op jit(solution)/shard_map/ppermute | solution.py:19
  64.1 1.9 collective-permute-start.6
  66.0 3.6 %collective-permute-start.7 = (bf16[32,34,1]{2,0,1:T(8,128)(2,1)S(1)}, bf16[32,34,1]{2,0,1:T(8,128)(2,1)S(1)}, u32[]{:S(2)}, u32[]{:S(2)}) collective-permute-start(bf16[32,34,1]{2,0,1:T(8,128)(2,1)S(1)} %get-tuple-element.14), channel_id=1, source_target_pairs={{1,0},{2,1},{3,2},{5,4},{6,5},{7,6},{9,8},{10,9},{11,10},{13,12},{... | collective-permute-start | bytes 6536 | tf_op jit(solution)/shard_map/ppermute | solution.py:19
  70.2 1.7 collective-permute-done.6
  71.9 1.8 collective-permute-done.7
  76.5 5.7 %slice.475 = bf16[32,16,128]{2,0,1:T(8,128)(2,1)S(1)} slice(bf16[32,32,256]{2,0,1:T(8,128)(2,1)S(1)} %get-tuple-element.70), slice={[0:32:1], [0:32:2], [0:256:2]} | slice | bytes 262144 | tf_op jit(solution)/shard_map/slice | solution.py:180
  82.2 5.7 %slice.477 = bf16[32,16,128]{2,0,1:T(8,128)(2,1)S(1)} slice(bf16[32,32,256]{2,0,1:T(8,128)(2,1)S(1)} %get-tuple-element.70), slice={[0:32:1], [0:32:2], [1:256:2]} | slice | bytes 262144 | tf_op jit(solution)/shard_map/slice | solution.py:180
  87.9 5.9 %slice.479 = bf16[32,16,128]{2,0,1:T(8,128)(2,1)S(1)} slice(bf16[32,32,256]{2,0,1:T(8,128)(2,1)S(1)} %get-tuple-element.70), slice={[0:32:1], [1:32:2], [0:256:2]} | slice | bytes 262144 | tf_op jit(solution)/shard_map/slice | solution.py:180
  93.8 5.9 %slice.481 = bf16[32,16,128]{2,0,1:T(8,128)(2,1)S(1)} slice(bf16[32,32,256]{2,0,1:T(8,128)(2,1)S(1)} %get-tuple-element.70), slice={[0:32:1], [1:32:2], [1:256:2]} | slice | bytes 262144 | tf_op jit(solution)/shard_map/slice | solution.py:180
  100.9 1.3 collective-permute-start.8
  102.2 4.8 %collective-permute-start.9 = (bf16[64,1,128]{2,0,1:T(8,128)(2,1)S(1)}, bf16[64,1,128]{2,0,1:T(8,128)(2,1)S(1)}, u32[]{:S(2)}, u32[]{:S(2)}) collective-permute-start(bf16[64,1,128]{2,0,1:T(8,128)(2,1)S(1)} %get-tuple-element.32), channel_id=1, source_target_pairs={{4,0},{8,4},{12,8},{5,1},{9,5},{13,9},{6,2},{10,6},{14,10},{7,3},{... | collective-permute-start | bytes 49160 | tf_op jit(solution)/shard_map/ppermute | solution.py:19
  108.7 1.9 collective-permute-start.10
  110.6 3.6 %collective-permute-start.11 = (bf16[64,18,1]{2,0,1:T(8,128)(2,1)S(1)}, bf16[64,18,1]{2,0,1:T(8,128)(2,1)S(1)}, u32[]{:S(2)}, u32[]{:S(2)}) collective-permute-start(bf16[64,18,1]{2,0,1:T(8,128)(2,1)S(1)} %get-tuple-element.28), channel_id=1, source_target_pairs={{1,0},{2,1},{3,2},{5,4},{6,5},{7,6},{9,8},{10,9},{11,10},{13,12},{... | collective-permute-start | bytes 6920 | tf_op jit(solution)/shard_map/ppermute | solution.py:19
  114.7 2.0 %collective-permute-done.10 = bf16[64,18,1]{2,0,1:T(8,128)(2,1)S(1)} collective-permute-done((bf16[64,18,1]{2,0,1:T(8,128)(2,1)S(1)}, bf16[64,18,1]{2,0,1:T(8,128)(2,1)S(1)}, u32[]{:S(2)}, u32[]{:S(2)}) %collective-permute-start.10) | collective-permute-done | bytes 2336 | tf_op jit(solution)/shard_map/ppermute | solution.py:16
  116.7 1.8 collective-permute-done.11
  121.4 4.2 %collective-permute-start.13 = (bf16[64,1,128]{2,0,1:T(8,128)(2,1)S(1)}, bf16[64,1,128]{2,0,1:T(8,128)(2,1)S(1)}, u32[]{:S(2)}, u32[]{:S(2)}) collective-permute-start(bf16[64,1,128]{2,0,1:T(8,128)(2,1)S(1)} %get-tuple-element.30), channel_id=1, source_target_pairs={{4,0},{8,4},{12,8},{5,1},{9,5},{13,9},{6,2},{10,6},{14,10},{7,3},{... | collective-permute-start | bytes 49160 | tf_op jit(solution)/shard_map/ppermute | solution.py:19
  125.6 1.5 collective-permute-start.12
  127.3 3.9 %collective-permute-done.12 = bf16[64,1,128]{2,0,1:T(8,128)(2,1)S(1)} collective-permute-done((bf16[64,1,128]{2,0,1:T(8,128)(2,1)S(1)}, bf16[64,1,128]{2,0,1:T(8,128)(2,1)S(1)}, u32[]{:S(2)}, u32[]{:S(2)}) %collective-permute-start.12) | collective-permute-done | bytes 16416 | tf_op jit(solution)/shard_map/ppermute | solution.py:16
  131.4 2.7 %collective-permute-start.14 = (bf16[64,18,1]{2,0,1:T(8,128)(2,1)S(1)}, bf16[64,18,1]{2,0,1:T(8,128)(2,1)S(1)}, u32[]{:S(2)}, u32[]{:S(2)}) collective-permute-start(bf16[64,18,1]{2,0,1:T(8,128)(2,1)S(1)} %get-tuple-element.23), channel_id=1, source_target_pairs={{1,0},{2,1},{3,2},{5,4},{6,5},{7,6},{9,8},{10,9},{11,10},{13,12},{... | collective-permute-start | bytes 6920 | tf_op jit(solution)/shard_map/ppermute | solution.py:19
  134.1 1.9 collective-permute-start.15
  136.6 1.7 collective-permute-done.14
  138.3 3.8 %collective-permute-done.15 = bf16[64,18,1]{2,0,1:T(8,128)(2,1)S(1)} collective-permute-done((bf16[64,18,1]{2,0,1:T(8,128)(2,1)S(1)}, bf16[64,18,1]{2,0,1:T(8,128)(2,1)S(1)}, u32[]{:S(2)}, u32[]{:S(2)}) %collective-permute-start.15) | collective-permute-done | bytes 2336 | tf_op jit(solution)/shard_map/ppermute | solution.py:16
  145.3 4.3 %copy.79 = f32[32,16,2,128,2]{0,4,3,2,1:T(2,128)} copy(f32[32,16,2,128,2]{3,0,1,4,2:T(8,128)S(1)} %pad_maximum_fusion) | data formatting | bytes 2097152 | tf_op jit(solution)/shard_map/stack | solution.py:214
  149.7 2.8 %copy.80 = f32[32,32,256]{2,0,1:T(8,128)S(1)} copy(f32[32,32,256]{0,2,1:T(8,128)} %bitcast.468) | data formatting | bytes 2097152 | tf_op jit(solution)/shard_map/reshape | solution.py:218
  152.9 3.9 %collective-permute-start.17 = (bf16[32,1,256]{2,0,1:T(8,128)(2,1)S(1)}, bf16[32,1,256]{2,0,1:T(8,128)(2,1)S(1)}, u32[]{:S(2)}, u32[]{:S(2)}) collective-permute-start(bf16[32,1,256]{2,0,1:T(8,128)(2,1)S(1)} %get-tuple-element.18), channel_id=1, source_target_pairs={{4,0},{8,4},{12,8},{5,1},{9,5},{13,9},{6,2},{10,6},{14,10},{7,3},{... | collective-permute-start | bytes 49160 | tf_op jit(solution)/shard_map/ppermute | solution.py:19
  156.8 1.3 collective-permute-start.16
  158.5 4.0 %collective-permute-done.16 = bf16[32,1,256]{2,0,1:T(8,128)(2,1)S(1)} collective-permute-done((bf16[32,1,256]{2,0,1:T(8,128)(2,1)S(1)}, bf16[32,1,256]{2,0,1:T(8,128)(2,1)S(1)}, u32[]{:S(2)}, u32[]{:S(2)}) %collective-permute-start.16) | collective-permute-done | bytes 16416 | tf_op jit(solution)/shard_map/ppermute | solution.py:16
  162.7 1.9 collective-permute-start.18
  164.6 2.4 %collective-permute-start.19 = (bf16[32,34,1]{2,0,1:T(8,128)(2,1)S(1)}, bf16[32,34,1]{2,0,1:T(8,128)(2,1)S(1)}, u32[]{:S(2)}, u32[]{:S(2)}) collective-permute-start(bf16[32,34,1]{2,0,1:T(8,128)(2,1)S(1)} %get-tuple-element.10), channel_id=1, source_target_pairs={{0,1},{1,2},{2,3},{4,5},{5,6},{6,7},{8,9},{9,10},{10,11},{12,13},{... | collective-permute-start | bytes 6536 | tf_op jit(solution)/shard_map/ppermute | solution.py:16
  168.6 3.8 %collective-permute-done.19 = bf16[32,34,1]{2,0,1:T(8,128)(2,1)S(1)} collective-permute-done((bf16[32,34,1]{2,0,1:T(8,128)(2,1)S(1)}, bf16[32,34,1]{2,0,1:T(8,128)(2,1)S(1)}, u32[]{:S(2)}, u32[]{:S(2)}) %collective-permute-start.19) | collective-permute-done | bytes 2208 | tf_op jit(solution)/shard_map/ppermute | solution.py:16
  174.9 1.3 fusion.15
  176.3 3.7 %collective-permute-start.21 = (bf16[32,1,256]{2,0,1:T(8,128)(2,1)S(1)}, bf16[32,1,256]{2,0,1:T(8,128)(2,1)S(1)}, u32[]{:S(2)}, u32[]{:S(2)}) collective-permute-start(bf16[32,1,256]{2,0,1:T(8,128)(2,1)S(1)} %get-tuple-element.16), channel_id=1, source_target_pairs={{4,0},{8,4},{12,8},{5,1},{9,5},{13,9},{6,2},{10,6},{14,10},{7,3},{... | collective-permute-start | bytes 49160 | tf_op jit(solution)/shard_map/ppermute | solution.py:19
  180.0 1.3 collective-permute-start.20
  181.5 4.1 %collective-permute-done.20 = bf16[32,1,256]{2,0,1:T(8,128)(2,1)S(1)} collective-permute-done((bf16[32,1,256]{2,0,1:T(8,128)(2,1)S(1)}, bf16[32,1,256]{2,0,1:T(8,128)(2,1)S(1)}, u32[]{:S(2)}, u32[]{:S(2)}) %collective-permute-start.20) | collective-permute-done | bytes 16416 | tf_op jit(solution)/shard_map/ppermute | solution.py:16
  185.8 1.9 collective-permute-start.22
  187.7 2.4 %collective-permute-start.23 = (bf16[32,34,1]{2,0,1:T(8,128)(2,1)S(1)}, bf16[32,34,1]{2,0,1:T(8,128)(2,1)S(1)}, u32[]{:S(2)}, u32[]{:S(2)}) collective-permute-start(bf16[32,34,1]{2,0,1:T(8,128)(2,1)S(1)} %get-tuple-element.6), channel_id=1, source_target_pairs={{0,1},{1,2},{2,3},{4,5},{5,6},{6,7},{8,9},{9,10},{10,11},{12,13},{... | collective-permute-start | bytes 6536 | tf_op jit(solution)/shard_map/ppermute | solution.py:16
  190.5 1.2 collective-permute-done.22
  191.8 3.8 %collective-permute-done.23 = bf16[32,34,1]{2,0,1:T(8,128)(2,1)S(1)} collective-permute-done((bf16[32,34,1]{2,0,1:T(8,128)(2,1)S(1)}, bf16[32,34,1]{2,0,1:T(8,128)(2,1)S(1)}, u32[]{:S(2)}, u32[]{:S(2)}) %collective-permute-start.23) | collective-permute-done | bytes 2208 | tf_op jit(solution)/shard_map/ppermute | solution.py:16
  (157 shorter events, 38.7 us)
Async XLA Ops:
  0.6 0.7 copy-start
  0.6 61.8 %copy-start.2 = (bf16[9,32,32]{2,1,0:T(8,128)(2,1)S(1)}, bf16[9,32,32]{2,1,0:T(8,128)(2,1)}, u32[]{:S(2)}) copy-start(bf16[9,32,32]{2,1,0:T(8,128)(2,1)} %param.14) | copy-start | bytes 55300
  16.1 7.3 %all-to-all-start = ((bf16[4,2,64]{2,1,0:T(2,128)(2,1)}), bf16[4,2,64]{2,1,0:T(2,128)(2,1)S(1)}, u32[]{:S(2)}, u32[]{:S(2)}) async-start(bf16[4,2,64]{2,1,0:T(2,128)(2,1)} %bitcast), calls=%async_computation | async-start | bytes 4096 | tf_op jit(solution)/shard_map/all_to_all | solution.py:149
  25.2 8.7 %all-to-all-start.1 = ((bf16[2,4,64]{2,0,1:T(2,128)(2,1)}), bf16[2,4,64]{2,0,1:T(2,128)(2,1)S(1)}, u32[]{:S(2)}, u32[]{:S(2)}) async-start(bf16[2,4,64]{2,0,1:T(2,128)(2,1)} %reshape.529), calls=%async_computation.1 | async-start | bytes 4096 | tf_op jit(solution)/shard_map/all_to_all | solution.py:159
  41.0 22.9 %copy-start.3 = (bf16[32,256]{1,0:T(8,128)(2,1)}, bf16[32,256]{1,0:T(8,128)(2,1)S(1)}, u32[]{:S(2)}) copy-start(bf16[32,256]{1,0:T(8,128)(2,1)S(1)} %get-tuple-element.69) | copy-start | bytes 49156
  41.0 7.2 %collective-permute-start = (bf16[1,1,256]{2,1,0:T(2,128)(2,1)S(1)}, bf16[1,1,256]{2,1,0:T(2,128)(2,1)S(1)}, u32[]{:S(2)}, u32[]{:S(2)}) collective-permute-start(bf16[1,1,256]{2,1,0:T(2,128)(2,1)S(1)} %get-tuple-element.45), channel_id=1, source_target_pairs={{0,4},{4,8},{8,12},{1,5},{5,9},{9,13},{2,6},{6,10},{10,14},{3,7},{... | collective-permute-start | bytes 1544 | tf_op jit(solution)/shard_map/ppermute | solution.py:16
  42.3 5.9 %collective-permute-start.1 = (bf16[1,1,256]{2,1,0:T(2,128)(2,1)S(1)}, bf16[1,1,256]{2,1,0:T(2,128)(2,1)S(1)}, u32[]{:S(2)}, u32[]{:S(2)}) collective-permute-start(bf16[1,1,256]{2,1,0:T(2,128)(2,1)S(1)} %get-tuple-element.46), channel_id=1, source_target_pairs={{4,0},{8,4},{12,8},{5,1},{9,5},{13,9},{6,2},{10,6},{14,10},{7,3},{... | collective-permute-start | bytes 1544 | tf_op jit(solution)/shard_map/ppermute | solution.py:19
  48.3 5.6 %collective-permute-start.2 = (bf16[1,34,1]{2,1,0:T(8,128)(2,1)S(1)}, bf16[1,34,1]{2,1,0:T(8,128)(2,1)S(1)}, u32[]{:S(2)}, u32[]{:S(2)}) collective-permute-start(bf16[1,34,1]{2,1,0:T(8,128)(2,1)S(1)} %get-tuple-element.39), channel_id=1, source_target_pairs={{0,1},{1,2},{2,3},{4,5},{5,6},{6,7},{8,9},{9,10},{10,11},{12,13},{... | collective-permute-start | bytes 212 | tf_op jit(solution)/shard_map/ppermute | solution.py:16
  50.2 5.0 %collective-permute-start.3 = (bf16[1,34,1]{2,1,0:T(8,128)(2,1)S(1)}, bf16[1,34,1]{2,1,0:T(8,128)(2,1)S(1)}, u32[]{:S(2)}, u32[]{:S(2)}) collective-permute-start(bf16[1,34,1]{2,1,0:T(8,128)(2,1)S(1)} %get-tuple-element.40), channel_id=1, source_target_pairs={{1,0},{2,1},{3,2},{5,4},{6,5},{7,6},{9,8},{10,9},{11,10},{13,12},{... | collective-permute-start | bytes 212 | tf_op jit(solution)/shard_map/ppermute | solution.py:19
  56.4 6.3 %collective-permute-start.4 = (bf16[32,1,256]{2,0,1:T(8,128)(2,1)S(1)}, bf16[32,1,256]{2,0,1:T(8,128)(2,1)S(1)}, u32[]{:S(2)}, u32[]{:S(2)}) collective-permute-start(bf16[32,1,256]{2,0,1:T(8,128)(2,1)S(1)} %get-tuple-element.19), channel_id=1, source_target_pairs={{0,4},{4,8},{8,12},{1,5},{5,9},{9,13},{2,6},{6,10},{10,14},{3,7},{... | collective-permute-start | bytes 49160 | tf_op jit(solution)/shard_map/ppermute | solution.py:16
  57.7 6.2 %collective-permute-start.5 = (bf16[32,1,256]{2,0,1:T(8,128)(2,1)S(1)}, bf16[32,1,256]{2,0,1:T(8,128)(2,1)S(1)}, u32[]{:S(2)}, u32[]{:S(2)}) collective-permute-start(bf16[32,1,256]{2,0,1:T(8,128)(2,1)S(1)} %get-tuple-element.20), channel_id=1, source_target_pairs={{4,0},{8,4},{12,8},{5,1},{9,5},{13,9},{6,2},{10,6},{14,10},{7,3},{... | collective-permute-start | bytes 49160 | tf_op jit(solution)/shard_map/ppermute | solution.py:19
  64.1 7.9 %collective-permute-start.6 = (bf16[32,34,1]{2,0,1:T(8,128)(2,1)S(1)}, bf16[32,34,1]{2,0,1:T(8,128)(2,1)S(1)}, u32[]{:S(2)}, u32[]{:S(2)}) collective-permute-start(bf16[32,34,1]{2,0,1:T(8,128)(2,1)S(1)} %get-tuple-element.13), channel_id=1, source_target_pairs={{0,1},{1,2},{2,3},{4,5},{5,6},{6,7},{8,9},{9,10},{10,11},{12,13},{... | collective-permute-start | bytes 6536 | tf_op jit(solution)/shard_map/ppermute | solution.py:16
  66.0 7.7 %collective-permute-start.7 = (bf16[32,34,1]{2,0,1:T(8,128)(2,1)S(1)}, bf16[32,34,1]{2,0,1:T(8,128)(2,1)S(1)}, u32[]{:S(2)}, u32[]{:S(2)}) collective-permute-start(bf16[32,34,1]{2,0,1:T(8,128)(2,1)S(1)} %get-tuple-element.14), channel_id=1, source_target_pairs={{1,0},{2,1},{3,2},{5,4},{6,5},{7,6},{9,8},{10,9},{11,10},{13,12},{... | collective-permute-start | bytes 6536 | tf_op jit(solution)/shard_map/ppermute | solution.py:19
  75.9 23.8 %copy-start.4 = (bf16[4,64,32]{1,2,0:T(8,128)(2,1)S(1)}, bf16[4,64,32]{1,2,0:T(8,128)(2,1)}, u32[]{:S(2)}) copy-start(bf16[4,64,32]{1,2,0:T(8,128)(2,1)} %param.15) | copy-start | bytes 49156
  100.3 6.8 %copy-start.1 = (bf16[9,64,64]{2,1,0:T(8,128)(2,1)S(1)}, bf16[9,64,64]{2,1,0:T(8,128)(2,1)}, u32[]{:S(2)}) copy-start(bf16[9,64,64]{2,1,0:T(8,128)(2,1)} %param.16) | copy-start | bytes 221188
  100.9 6.3 %collective-permute-start.8 = (bf16[64,1,128]{2,0,1:T(8,128)(2,1)S(1)}, bf16[64,1,128]{2,0,1:T(8,128)(2,1)S(1)}, u32[]{:S(2)}, u32[]{:S(2)}) collective-permute-start(bf16[64,1,128]{2,0,1:T(8,128)(2,1)S(1)} %get-tuple-element.31), channel_id=1, source_target_pairs={{0,4},{4,8},{8,12},{1,5},{5,9},{9,13},{2,6},{6,10},{10,14},{3,7},{... | collective-permute-start | bytes 49160 | tf_op jit(solution)/shard_map/ppermute | solution.py:16
  102.2 6.2 %collective-permute-start.9 = (bf16[64,1,128]{2,0,1:T(8,128)(2,1)S(1)}, bf16[64,1,128]{2,0,1:T(8,128)(2,1)S(1)}, u32[]{:S(2)}, u32[]{:S(2)}) collective-permute-start(bf16[64,1,128]{2,0,1:T(8,128)(2,1)S(1)} %get-tuple-element.32), channel_id=1, source_target_pairs={{4,0},{8,4},{12,8},{5,1},{9,5},{13,9},{6,2},{10,6},{14,10},{7,3},{... | collective-permute-start | bytes 49160 | tf_op jit(solution)/shard_map/ppermute | solution.py:19
  108.7 8.0 %collective-permute-start.10 = (bf16[64,18,1]{2,0,1:T(8,128)(2,1)S(1)}, bf16[64,18,1]{2,0,1:T(8,128)(2,1)S(1)}, u32[]{:S(2)}, u32[]{:S(2)}) collective-permute-start(bf16[64,18,1]{2,0,1:T(8,128)(2,1)S(1)} %get-tuple-element.27), channel_id=1, source_target_pairs={{0,1},{1,2},{2,3},{4,5},{5,6},{6,7},{8,9},{9,10},{10,11},{12,13},{... | collective-permute-start | bytes 6920 | tf_op jit(solution)/shard_map/ppermute | solution.py:16
  110.6 7.9 %collective-permute-start.11 = (bf16[64,18,1]{2,0,1:T(8,128)(2,1)S(1)}, bf16[64,18,1]{2,0,1:T(8,128)(2,1)S(1)}, u32[]{:S(2)}, u32[]{:S(2)}) collective-permute-start(bf16[64,18,1]{2,0,1:T(8,128)(2,1)S(1)} %get-tuple-element.28), channel_id=1, source_target_pairs={{1,0},{2,1},{3,2},{5,4},{6,5},{7,6},{9,8},{10,9},{11,10},{13,12},{... | collective-permute-start | bytes 6920 | tf_op jit(solution)/shard_map/ppermute | solution.py:19
  120.1 0.7 copy-start.7
  121.0 10.4 %copy-start.6 = (f32[1,16,128]{2,0,1:T(1,128)}, f32[1,16,128]{2,0,1:T(1,128)S(1)}, u32[]{:S(2)}) copy-start(f32[1,16,128]{2,0,1:T(1,128)S(1)} %fusion.130) | copy-start | bytes 24580
  121.4 6.0 %collective-permute-start.13 = (bf16[64,1,128]{2,0,1:T(8,128)(2,1)S(1)}, bf16[64,1,128]{2,0,1:T(8,128)(2,1)S(1)}, u32[]{:S(2)}, u32[]{:S(2)}) collective-permute-start(bf16[64,1,128]{2,0,1:T(8,128)(2,1)S(1)} %get-tuple-element.30), channel_id=1, source_target_pairs={{4,0},{8,4},{12,8},{5,1},{9,5},{13,9},{6,2},{10,6},{14,10},{7,3},{... | collective-permute-start | bytes 49160 | tf_op jit(solution)/shard_map/ppermute | solution.py:19
  125.6 5.6 %collective-permute-start.12 = (bf16[64,1,128]{2,0,1:T(8,128)(2,1)S(1)}, bf16[64,1,128]{2,0,1:T(8,128)(2,1)S(1)}, u32[]{:S(2)}, u32[]{:S(2)}) collective-permute-start(bf16[64,1,128]{2,0,1:T(8,128)(2,1)S(1)} %get-tuple-element.29), channel_id=1, source_target_pairs={{0,4},{4,8},{8,12},{1,5},{5,9},{9,13},{2,6},{6,10},{10,14},{3,7},{... | collective-permute-start | bytes 49160 | tf_op jit(solution)/shard_map/ppermute | solution.py:16
  131.4 6.9 %collective-permute-start.14 = (bf16[64,18,1]{2,0,1:T(8,128)(2,1)S(1)}, bf16[64,18,1]{2,0,1:T(8,128)(2,1)S(1)}, u32[]{:S(2)}, u32[]{:S(2)}) collective-permute-start(bf16[64,18,1]{2,0,1:T(8,128)(2,1)S(1)} %get-tuple-element.23), channel_id=1, source_target_pairs={{1,0},{2,1},{3,2},{5,4},{6,5},{7,6},{9,8},{10,9},{11,10},{13,12},{... | collective-permute-start | bytes 6920 | tf_op jit(solution)/shard_map/ppermute | solution.py:19
  134.1 8.0 %collective-permute-start.15 = (bf16[64,18,1]{2,0,1:T(8,128)(2,1)S(1)}, bf16[64,18,1]{2,0,1:T(8,128)(2,1)S(1)}, u32[]{:S(2)}, u32[]{:S(2)}) collective-permute-start(bf16[64,18,1]{2,0,1:T(8,128)(2,1)S(1)} %get-tuple-element.24), channel_id=1, source_target_pairs={{0,1},{1,2},{2,3},{4,5},{5,6},{6,7},{8,9},{9,10},{10,11},{12,13},{... | collective-permute-start | bytes 6920 | tf_op jit(solution)/shard_map/ppermute | solution.py:16
  152.9 5.6 %collective-permute-start.17 = (bf16[32,1,256]{2,0,1:T(8,128)(2,1)S(1)}, bf16[32,1,256]{2,0,1:T(8,128)(2,1)S(1)}, u32[]{:S(2)}, u32[]{:S(2)}) collective-permute-start(bf16[32,1,256]{2,0,1:T(8,128)(2,1)S(1)} %get-tuple-element.18), channel_id=1, source_target_pairs={{4,0},{8,4},{12,8},{5,1},{9,5},{13,9},{6,2},{10,6},{14,10},{7,3},{... | collective-permute-start | bytes 49160 | tf_op jit(solution)/shard_map/ppermute | solution.py:19
  156.8 5.6 %collective-permute-start.16 = (bf16[32,1,256]{2,0,1:T(8,128)(2,1)S(1)}, bf16[32,1,256]{2,0,1:T(8,128)(2,1)S(1)}, u32[]{:S(2)}, u32[]{:S(2)}) collective-permute-start(bf16[32,1,256]{2,0,1:T(8,128)(2,1)S(1)} %get-tuple-element.17), channel_id=1, source_target_pairs={{0,4},{4,8},{8,12},{1,5},{5,9},{9,13},{2,6},{6,10},{10,14},{3,7},{... | collective-permute-start | bytes 49160 | tf_op jit(solution)/shard_map/ppermute | solution.py:16
  162.7 6.0 %collective-permute-start.18 = (bf16[32,34,1]{2,0,1:T(8,128)(2,1)S(1)}, bf16[32,34,1]{2,0,1:T(8,128)(2,1)S(1)}, u32[]{:S(2)}, u32[]{:S(2)}) collective-permute-start(bf16[32,34,1]{2,0,1:T(8,128)(2,1)S(1)} %get-tuple-element.9), channel_id=1, source_target_pairs={{1,0},{2,1},{3,2},{5,4},{6,5},{7,6},{9,8},{10,9},{11,10},{13,12},{... | collective-permute-start | bytes 6536 | tf_op jit(solution)/shard_map/ppermute | solution.py:19
  164.6 7.9 %collective-permute-start.19 = (bf16[32,34,1]{2,0,1:T(8,128)(2,1)S(1)}, bf16[32,34,1]{2,0,1:T(8,128)(2,1)S(1)}, u32[]{:S(2)}, u32[]{:S(2)}) collective-permute-start(bf16[32,34,1]{2,0,1:T(8,128)(2,1)S(1)} %get-tuple-element.10), channel_id=1, source_target_pairs={{0,1},{1,2},{2,3},{4,5},{5,6},{6,7},{8,9},{9,10},{10,11},{12,13},{... | collective-permute-start | bytes 6536 | tf_op jit(solution)/shard_map/ppermute | solution.py:16
  174.9 6.3 %copy-start.5 = (bf16[9,32]{1,0:T(8,128)(2,1)S(1)}, bf16[9,32]{1,0:T(8,128)(2,1)}, u32[]{:S(2)}) copy-start(bf16[9,32]{1,0:T(8,128)(2,1)} %param.13) | copy-start | bytes 1732
  176.3 5.2 %collective-permute-start.21 = (bf16[32,1,256]{2,0,1:T(8,128)(2,1)S(1)}, bf16[32,1,256]{2,0,1:T(8,128)(2,1)S(1)}, u32[]{:S(2)}, u32[]{:S(2)}) collective-permute-start(bf16[32,1,256]{2,0,1:T(8,128)(2,1)S(1)} %get-tuple-element.16), channel_id=1, source_target_pairs={{4,0},{8,4},{12,8},{5,1},{9,5},{13,9},{6,2},{10,6},{14,10},{7,3},{... | collective-permute-start | bytes 49160 | tf_op jit(solution)/shard_map/ppermute | solution.py:19
  180.0 5.6 %collective-permute-start.20 = (bf16[32,1,256]{2,0,1:T(8,128)(2,1)S(1)}, bf16[32,1,256]{2,0,1:T(8,128)(2,1)S(1)}, u32[]{:S(2)}, u32[]{:S(2)}) collective-permute-start(bf16[32,1,256]{2,0,1:T(8,128)(2,1)S(1)} %get-tuple-element.15), channel_id=1, source_target_pairs={{0,4},{4,8},{8,12},{1,5},{5,9},{9,13},{2,6},{6,10},{10,14},{3,7},{... | collective-permute-start | bytes 49160 | tf_op jit(solution)/shard_map/ppermute | solution.py:16
  185.8 6.0 %collective-permute-start.22 = (bf16[32,34,1]{2,0,1:T(8,128)(2,1)S(1)}, bf16[32,34,1]{2,0,1:T(8,128)(2,1)S(1)}, u32[]{:S(2)}, u32[]{:S(2)}) collective-permute-start(bf16[32,34,1]{2,0,1:T(8,128)(2,1)S(1)} %get-tuple-element.5), channel_id=1, source_target_pairs={{1,0},{2,1},{3,2},{5,4},{6,5},{7,6},{9,8},{10,9},{11,10},{13,12},{... | collective-permute-start | bytes 6536 | tf_op jit(solution)/shard_map/ppermute | solution.py:19
  187.7 7.9 %collective-permute-start.23 = (bf16[32,34,1]{2,0,1:T(8,128)(2,1)S(1)}, bf16[32,34,1]{2,0,1:T(8,128)(2,1)S(1)}, u32[]{:S(2)}, u32[]{:S(2)}) collective-permute-start(bf16[32,34,1]{2,0,1:T(8,128)(2,1)S(1)} %get-tuple-element.6), channel_id=1, source_target_pairs={{0,1},{1,2},{2,3},{4,5},{5,6},{6,7},{8,9},{9,10},{10,11},{12,13},{... | collective-permute-start | bytes 6536 | tf_op jit(solution)/shard_map/ppermute | solution.py:16
where the time goes:
time: 199 us; the launch traced here: 198 us
  starting transfers between devices  75.3 us (38%)
  waiting for transfers between devices  40.1 us (20%)
  local copies, waits for them, and re-layouts  35.7 us (18%)
  matrix products  21.3 us (11%)
  blocking collectives  15.4 us (8%)
  other arithmetic  8.27 us (4%)
  between operations  2.24 us (1%)
    ppermute x12, starting transfers between devices, with_halo(): lax.ppermute(lax.slice_in_dim(block, 0, width, axis=dim), axis, backward)  43.3 us
    ppermute x12, waiting for transfers between devices, with_halo(): lax.ppermute(lax.slice_in_dim(block, block.shape[dim] - width, None, axis...  27.2 us
    slice x4, local copies, waits for them, and re-layouts, local(): window = act_second[:, shift_row::2, shift_col::2]  23.2 us
    ppermute x12, starting transfers between devices, with_halo(): lax.ppermute(lax.slice_in_dim(block, block.shape[dim] - width, None, axis...  20.4 us
    ppermute x12, waiting for transfers between devices, with_halo(): lax.ppermute(lax.slice_in_dim(block, 0, width, axis=dim), axis, backward)  11.1 us
    unnamed x1, blocking collectives  10.2 us
    dot_general x27, matrix products, conv_backward(): jnp.einsum('oi,ohw->ihw', weight[kernel_tap], window, preferred_element_t...  9.13 us
    all_to_all x1, starting transfers between devices, local(): lax.all_to_all(outgoing, 'ch', split_axis=1, concat_axis=0, tiled=True)  6.45 us
  transfers between devices with their start and end apart: 26, of which 18 were waited for; matrix products, arithmetic and copies ran while one was open for 4% of the time, Pallas kernels for 0%

commit v1 on v0

v1 whole, which is shorter than its diff:
```python
import functools
import math

import jax
import jax.numpy as jnp
from jax import lax
from jax.experimental import pallas as pl
from jax.experimental.pallas import tpu as pltpu
from jax.sharding import PartitionSpec as P

SIGMA = 64
HALO = 4
MARGIN = 256
F32 = jnp.float32
BF16 = jnp.bfloat16
SHIFTS = [(sy, sx) for sy in (-1, 0, 1) for sx in (-1, 0, 1)]
PATCH = [(y, x) for y in (-1, 0, 1, 2) for x in (-1, 0, 1, 2)]


def mm(lhs, rhs):
    return jnp.dot(lhs, rhs, preferred_element_type=F32)


def mm_nt(lhs, rhs):
    return lax.dot_general(lhs, rhs, (((1,), (1,)), ((), ())), preferred_element_type=F32)


def split(value):
    high = value.astype(BF16)
    return high, (value - high.astype(F32)).astype(BF16)


def cosine_turns(count, samples):
    folded = jnp.abs(count - samples // 2).astype(F32)
    z = folded * (2.0 * math.pi / samples) - (math.pi / 2)
    z2 = z * z
    poly = jnp.full_like(z2, -1.0 / 39916800)
    for term in (362880, -5040, 120, -6, 1):
        poly = poly * z2 + 1.0 / term
    return z * poly


def table(freq_row, freqs, first_time, step, length, samples):
    time = first_time + step * lax.broadcasted_iota(jnp.int32, (length, 2 * freqs), 0)
    lane = lax.broadcasted_iota(jnp.int32, (length, 2 * freqs), 1)
    quarter = jnp.where(lane >= freqs, samples // 4, 0)
    return cosine_turns((freq_row * time + quarter) & (samples - 1), samples)


def silu_parts(v):
    s = 0.5 * jnp.tanh(0.5 * v) + 0.5
    y = v * s
    return y, s + y * (1.0 - s)


class Geometry:
    def __init__(self, rows, cols):
        self.rows, self.cols = rows, cols
        self.high = rows + 2 * HALO
        self.pitch = cols + 2 * HALO
        self.size = self.high * self.pitch
        self.padded = -(-self.size // 256) * 256
        self.width = self.padded + 2 * MARGIN
        count = 2
        tiles = self.padded // 128
        self.chunks = []
        at = 0
        for i in range(count):
            end = tiles * (i + 1) // count
            self.chunks.append((at * 128, (end - at) * 128))
            at = end

    def offset(self, sy, sx):
        return sy * self.pitch + sx


def unet(geo, samples, total_rows, pb, freq_row, freqs, pick_col, me_ch, me_t, refs, outs, scr):
    w1_ref, w2_ref, ws_ref, w3_ref, wh_ref = refs
    filt_o, logit_o, grad_o = outs
    x0, mask_s, targ_s, act1, sl1, sl2, act_s, sls, dl3, dl2, zs, log_s, grad_s, un = scr
    rows, cols, pitch = geo.rows, geo.cols, geo.pitch
    total_cols = samples // 2
    scale = 2.0 / samples
    f1 = w2_ref.shape[1]
    for ref in (x0, act1, act_s, dl3, dl2, zs):
        n = ref.shape[0]
        ref[:, :MARGIN] = jnp.zeros((n, MARGIN), ref.dtype)
        ref[:, MARGIN + geo.padded :] = jnp.zeros((n, MARGIN), ref.dtype)
    place = lax.broadcasted_iota(jnp.int32, (8, geo.padded), 1).astype(F32)[:1]
    row = jnp.floor((place + 0.5) * (1.0 / pitch))
    col = place - row * pitch
    grow = row + (me_ch * rows - HALO).astype(F32)
    gcol = col + (me_t * cols - HALO).astype(F32)
    inside = (grow >= 0) & (grow < total_rows) & (gcol >= 0) & (gcol < total_cols) & (row < geo.high)
    mask = jnp.where(inside, 1.0, 0.0)
    mask_s[...] = jnp.broadcast_to(mask, mask_s.shape)
    rid = lax.broadcasted_iota(jnp.int32, (geo.high, geo.padded), 0).astype(F32)
    pick = jnp.sum(jnp.where(rid == row, pick_col, 0.0), axis=0, keepdims=True)
    offs = (2.0 * gcol - pick) * (1.0 / SIGMA)
    targ_s[...] = jnp.broadcast_to(jnp.exp(-0.5 * offs * offs), targ_s.shape)
    w2 = [w2_ref[k].astype(F32) for k in range(9)]
    zero = jnp.zeros_like(w2[0])

    def tap(y, x, a, b, sign):
        ky, kx = sign * (y - a) + 1, sign * (x - b) + 1
        return w2[3 * ky + kx] if 0 <= ky < 3 and 0 <= kx < 3 else zero

    phases = [(a, b) for a in (0, 1) for b in (0, 1)]
    w2_f = jnp.concatenate(
        [jnp.concatenate([tap(y, x, a, b, 1) for y, x in PATCH], axis=1) for a, b in phases], axis=0
    ).astype(BF16)
    w2_b = jnp.concatenate(
        [jnp.concatenate([tap(y, x, a, b, -1) for a, b in phases], axis=1) for y, x in PATCH], axis=0
    ).T.astype(BF16)
    ws_f32 = jnp.concatenate([ws_ref[k].astype(F32) for k in range(4)], axis=1)
    ws_f, ws_b = ws_f32.astype(BF16), ws_f32.T.astype(BF16)
    w3 = [w3_ref[k].astype(F32) for k in range(9)]
    w3_f = jnp.concatenate(w3, axis=1).astype(BF16)
    w3_b = jnp.concatenate(w3, axis=0).T.astype(BF16)
    head = jnp.broadcast_to(wh_ref[...].astype(F32), (8, wh_ref.shape[1]))
    head_col = head.T[:, :1]
    head_row = head.astype(BF16)
    srow = lax.broadcasted_iota(jnp.int32, (72, 9), 0)
    tapi = lax.broadcasted_iota(jnp.int32, (72, 9), 1)
    w1 = w1_ref[...]
    parts = []
    for a, b in phases:
        sel = jnp.zeros((72, 9), F32)
        for s, (sy, sx) in enumerate(SHIFTS):
            for p, (py, px) in enumerate(phases):
                ky, kx = 2 * sy + py - a + 1, 2 * sx + px - b + 1
                if 0 <= ky < 3 and 0 <= kx < 3:
                    sel = jnp.where((srow == 8 * s + p) & (tapi == 3 * ky + kx), 1.0, sel)
        parts.append(mm(sel.astype(BF16), w1))
    w1_b32 = jnp.concatenate(parts, axis=1)
    w1_f, w1_b = w1_b32.T.astype(BF16), w1_b32.astype(BF16)

    nat_h, nat_l = split(table(freq_row, freqs, me_t * 2 * cols, 1, 2 * cols, samples))
    nat = (mm_nt(pb, nat_h) + mm_nt(pb, nat_l)) * scale
    filt_o[...] = nat[2 * HALO : 2 * HALO + 2 * rows].astype(BF16)
    x0[...] = jnp.zeros_like(x0)
    for b in range(2):
        t_h, t_l = split(
            table(freq_row, freqs, me_t * 2 * cols - 2 * HALO + b, 2, geo.pitch, samples)
        )
        un[:, :pitch] = (mm_nt(pb, t_h) + mm_nt(pb, t_l)) * scale
        for r in range(geo.high):
            at = MARGIN + r * pitch
            for a in range(2):
                x0[2 * a + b : 2 * a + b + 1, at : at + pitch] = un[2 * r + a : 2 * r + a + 1, :pitch]
    x0[:, MARGIN : MARGIN + geo.padded] = x0[:, MARGIN : MARGIN + geo.padded] * mask_s[...]

    for at, n in geo.chunks:
        patches = jnp.concatenate(
            [x0[:, MARGIN + at + geo.offset(*s) : MARGIN + at + geo.offset(*s) + n] for s in SHIFTS], axis=0
        ).astype(BF16)
        y, slope = silu_parts(mm(w1_f, patches))
        act1[:, MARGIN + at : MARGIN + at + n] = (y * mask_s[:1, at : at + n]).astype(BF16)
        sl1[:, at : at + n] = slope

    def fine_patches(ref, at, n):
        blocks = []
        for y, x in PATCH:
            p = 2 * (y % 2) + x % 2
            start = MARGIN + at + geo.offset(y // 2, x // 2)
            blocks.append(ref[p * f1 : (p + 1) * f1, start : start + n])
        return jnp.concatenate(blocks, axis=0)

    def coarse_patches(ref, at, n, sign):
        blocks = []
        for s in SHIFTS:
            start = MARGIN + at + sign * geo.offset(*s)
            blocks.append(ref[:, start : start + n])
        return jnp.concatenate(blocks, axis=0)

    for at, n in geo.chunks:
        y, slope = silu_parts(mm(w2_f, fine_patches(act1, at, n)))
        sl2[:, at : at + n] = slope
        y, slope = silu_parts(mm(ws_f, y.astype(BF16)))
        act_s[:, MARGIN + at : MARGIN + at + n] = (y * mask_s[:1, at : at + n]).astype(BF16)
        sls[:, at : at + n] = slope
    for at, n in geo.chunks:
        y, slope = silu_parts(mm(w3_f, coarse_patches(act_s, at, n, 1)))
        logits = mm(head_row, y.astype(BF16))
        log_s[:, at : at + n] = logits
        out = (0.5 * jnp.tanh(0.5 * logits) + 0.5 - targ_s[:, at : at + n]) * mask_s[:, at : at + n]
        dl3[:, MARGIN + at : MARGIN + at + n] = (head_col * out[:1] * slope).astype(BF16)
    for at, n in geo.chunks:
        back = mm(w3_b, coarse_patches(dl3, at, n, -1))
        back = mm(ws_b, (back * sls[:, at : at + n]).astype(BF16))
        dl2[:, MARGIN + at : MARGIN + at + n] = (
            back * sl2[:, at : at + n] * mask_s[:1, at : at + n]
        ).astype(BF16)
    for at, n in geo.chunks:
        back = mm(w2_b, fine_patches(dl2, at, n))
        delta = (back * sl1[:, at : at + n] * mask_s[:1, at : at + n]).astype(BF16)
        zs[:, MARGIN + at : MARGIN + at + n] = mm(w1_b, delta)
    for at, n in geo.chunks:
        total = None
        for s, shift in enumerate(SHIFTS):
            start = MARGIN + at - geo.offset(*shift)
            term = zs[8 * s : 8 * s + 8, start : start + n]
            total = term if total is None else total + term
        grad_s[:, at : at + n] = total
    for r in range(rows):
        at = (r + HALO) * pitch + HALO
        logit_o[r : r + 1, :] = log_s[:1, at : at + cols]
    spread = None
    lane = lax.broadcasted_iota(jnp.int32, (cols, 2 * cols), 1)
    sub = lax.broadcasted_iota(jnp.int32, (cols, 2 * cols), 0)
    for b in range(2):
        for r in range(rows):
            at = (r + HALO) * pitch + HALO
            for a in range(2):
                un[2 * r + a : 2 * r + a + 1, :cols] = grad_s[2 * a + b : 2 * a + b + 1, at : at + cols]
        g_h, g_l = split(un[: 2 * rows, :cols])
        place = jnp.where(lane == 2 * sub + b, 1.0, 0.0).astype(BF16)
        term = mm(g_h, place) + mm(g_l, place)
        spread = term if spread is None else spread + term
    grad_o[...] = spread


def unet_scratch(geo, f1, f2):
    return [
        pltpu.VMEM((8, geo.width), F32),
        pltpu.VMEM((8, geo.padded), F32),
        pltpu.VMEM((8, geo.padded), F32),
        pltpu.VMEM((4 * f1, geo.width), BF16),
        pltpu.VMEM((4 * f1, geo.padded), F32),
        pltpu.VMEM((4 * f1, geo.padded), F32),
        pltpu.VMEM((f2, geo.width), BF16),
        pltpu.VMEM((f2, geo.padded), F32),
        pltpu.VMEM((f2, geo.width), BF16),
        pltpu.VMEM((4 * f1, geo.width), BF16),
        pltpu.VMEM((72, geo.width), F32),
        pltpu.VMEM((8, geo.padded), F32),
        pltpu.VMEM((8, geo.padded), F32),
        pltpu.VMEM((2 * geo.high, -(-geo.pitch // 128) * 128), F32),
    ]


def out_shapes(geo):
    return (
        jax.ShapeDtypeStruct((2 * geo.rows, 2 * geo.cols), BF16),
        jax.ShapeDtypeStruct((geo.rows, geo.cols), F32),
        jax.ShapeDtypeStruct((2 * geo.rows, 2 * geo.cols), F32),
    )


def step_kernel(geo, samples, total_rows, freqs, pb, freq, pick, w1, w2, ws, w3, wh, *rest):
    me_ch, me_t = lax.axis_index("ch"), lax.axis_index("tm") * lax.axis_size("sub") + lax.axis_index("sub")
    unet(
        geo, samples, total_rows, pb[...], freq[...], freqs, pick[...], me_ch, me_t,
        (w1, w2, ws, w3, wh), rest[:3], rest[3:],
    )


def wave_tables(total, channels_out=None):
    index = jnp.arange(total, dtype=jnp.int32)
    angle = (index[:, None] * index[None, :] % total).astype(F32) * (2.0 * math.pi / total)
    return jnp.cos(angle), jnp.sin(angle)


def spectral_wide(record, freq_bins, wave_limit, geo, samples, total_chans):
    precise = lax.Precision.HIGHEST
    local_chans, local_times = record.shape
    chan_groups = lax.axis_size("ch")
    time_groups = lax.axis_size(("tm", "sub"))
    freq_count = freq_bins.shape[0]
    bins_local = freq_count // (chan_groups * time_groups)
    time_index = lax.axis_index(("tm", "sub")) * local_times + jnp.arange(local_times, dtype=jnp.int32)
    angle = (freq_bins[:, None] * time_index[None, :] % samples).astype(F32) * (2.0 * math.pi / samples)
    signal = record.astype(F32)
    real_part = jnp.einsum("ft,ct->fc", jnp.cos(angle), signal, precision=precise)
    imag_part = -jnp.einsum("ft,ct->fc", jnp.sin(angle), signal, precision=precise)
    summed = lax.psum_scatter(
        jnp.concatenate([real_part, imag_part], axis=1), ("tm", "sub"), scatter_dimension=0, tiled=True
    )
    gathered = lax.all_to_all(summed.astype(BF16), "ch", split_axis=0, concat_axis=1, tiled=True)
    block = lax.axis_index(("tm", "sub")) * chan_groups + lax.axis_index("ch")
    arranged = gathered.reshape(bins_local, chan_groups, 2, local_chans).transpose(2, 0, 1, 3)
    arranged = arranged.reshape(2, bins_local, total_chans).astype(F32)
    limits = lax.dynamic_slice_in_dim(wave_limit, block * bins_local, bins_local)
    cosine, sine = wave_tables(total_chans)
    dot = functools.partial(jnp.dot, precision=precise)
    re = dot(arranged[0], cosine) + dot(arranged[1], sine)
    im = dot(arranged[1], cosine) - dot(arranged[0], sine)
    index = jnp.arange(total_chans, dtype=jnp.int32)
    passing = jnp.minimum(index, total_chans - index)[None] <= limits[:, None]
    re, im = jnp.where(passing, re, 0.0), jnp.where(passing, im, 0.0)
    out = jnp.stack([dot(re, cosine) - dot(im, sine), dot(im, cosine) + dot(re, sine)]) / total_chans
    out = jnp.pad(out.astype(BF16), ((0, 0), (0, 0), (2 * HALO, 2 * HALO)))
    wide = local_chans + 4 * HALO
    outgoing = jnp.stack([out[:, :, g * local_chans : g * local_chans + wide] for g in range(chan_groups)])
    outgoing = outgoing.transpose(2, 0, 1, 3).reshape(bins_local, chan_groups * 2 * wide)
    returned = lax.all_to_all(outgoing, "ch", split_axis=1, concat_axis=0, tiled=True)
    values = lax.all_gather(returned, ("tm", "sub"), axis=0, tiled=True)
    return values.reshape(freq_count, 2, wide).transpose(2, 1, 0).reshape(wide, 2 * freq_count)


def local(record, freq_bins, wave_limit, pick_index, w1, w2, ws, w3, wh):
    local_chans, local_times = record.shape
    chan_groups = lax.axis_size("ch")
    samples = local_times * lax.axis_size(("tm", "sub"))
    total_chans = local_chans * chan_groups
    freqs = freq_bins.shape[0]
    geo = Geometry(local_chans // 2, local_times // 2)
    pb = spectral_wide(record, freq_bins, wave_limit, geo, samples, total_chans)
    freq_row = jnp.concatenate([freq_bins, freq_bins])[None]
    picks = jnp.pad(lax.all_gather(pick_index, "ch", axis=0, tiled=True), (HALO, HALO))
    picks = lax.dynamic_slice_in_dim(picks, lax.axis_index("ch") * geo.rows, geo.high)
    vmem = pl.BlockSpec(memory_space=pltpu.VMEM)
    return pl.pallas_call(
        functools.partial(step_kernel, geo, samples, total_chans // 2, freqs),
        out_shape=out_shapes(geo),
        in_specs=[vmem] * 8,
        out_specs=(vmem,) * 3,
        scratch_shapes=unet_scratch(geo, w2.shape[1], w3.shape[1]),
        compiler_params=pltpu.CompilerParams(vmem_limit_bytes=48 * 2**20),
    )(pb, freq_row, picks.astype(F32)[:, None], w1, w2, ws, w3, wh[None])


def solution(mesh):
    return jax.shard_map(
        local,
        mesh=mesh,
        in_specs=(
            P(("grp", "ch"), ("tm", "sub")),
            P("grp"),
            P("grp"),
            P(("grp", "ch")),
            P(),
            P(),
            P(),
            P(),
            P(),
        ),
        out_specs=(P(("grp", "ch"), ("tm", "sub")),) * 3,
        check_vma=False,
    )
```

time: 199 us -> 65.7 us (0.33)
  the two profiles are of different devices: /device:TPU:26 before, /device:TPU:0 now
where the time goes in v1:
time: 65.7 us; the launch traced here: 65.3 us
  blocking collectives  26.8 us (41%)
  Pallas kernels  12.1 us (18%)
  starting transfers between devices  8.09 us (12%)
  local copies, waits for them, and re-layouts  6.72 us (10%)
  waiting for transfers between devices  5.14 us (8%)
  matrix products  3.99 us (6%)
  between operations  2.11 us (3%)
    unnamed x2, blocking collectives  21.4 us
    pallas_call x1, Pallas kernels, local(): pl.pallas_call(functools.partial(step_kernel, geo, samples, total_chans /...  12.1 us
    all_gather x1, blocking collectives, spectral_wide(): values = lax.all_gather(returned, ('tm', 'sub'), axis=0, tiled=True)  5.33 us
    all_to_all x1, waiting for transfers between devices, spectral_wide(): lax.all_to_all(outgoing, 'ch', split_axis=1, concat_axis=0, tiled=True)  5.14 us
    all_to_all x1, starting transfers between devices, spectral_wide(): lax.all_to_all(summed.astype(BF16), 'ch', split_axis=0, concat_axis=1, ti...  4.87 us
    unnamed x27, local copies, waits for them, and re-layouts  4.76 us
    all_to_all x1, starting transfers between devices, spectral_wide(): lax.all_to_all(outgoing, 'ch', split_axis=1, concat_axis=0, tiled=True)  3.22 us
  transfers between devices with their start and end apart: 2, of which 1 were waited for; matrix products, arithmetic and copies ran while one was open for 2% of the time, Pallas kernels for 0%

profile of v1, /device:TPU:0, one launch (start us, length us, event | category | flops | bytes accessed | tf_op | source)
XLA Modules:
  0.0 65.3 jit_solution(12709656663796425894)
XLA Ops:
  0.6 0.0 copy-start
  0.7 0.0 copy-start.6
  0.7 0.7 %copy-done = bf16[32,256]{1,0:T(8,128)(2,1)S(1)} copy-done((bf16[32,256]{1,0:T(8,128)(2,1)S(1)}, bf16[32,256]{1,0:T(8,128)(2,1)}, u32[]{:S(2)}) %copy-start) | copy-done | bytes 16408
  1.4 0.0 copy-done.6
  1.4 0.3 convolution_negate_fusion
  1.7 0.3 fusion.28
  2.0 0.1 pad_maximum_fusion
  2.1 12.7 %all-reduce.3 = bf16[32,64]{1,0:T(8,128)(2,1)S(1)} all-reduce(f32[32,64]{1,0:T(8,128)S(1)} %pad_maximum_fusion), channel_id=2, replica_groups=mesh['grp'=2,'ch'=4,'tm'=2,'sub'=2] {'tm','sub'}, use_global_device_ids=true, to_apply=%region_0.1.clone | all-reduce | flops 2048 | bytes 12288
  14.8 0.7 %copy-done.10 = u32[32]{0:T(128)S(1)} copy-done((u32[32]{0:T(128)S(1)}, u32[32]{0:T(128)}, u32[]{:S(2)}) %copy-start.10) | copy-done | bytes 152
  15.4 0.6 dynamic-slice.1
  16.7 0.6 dynamic-slice_convert_fusion
  17.2 4.9 %all-to-all-start = ((bf16[4,2,64]{2,1,0:T(2,128)(2,1)}), bf16[4,2,64]{2,1,0:T(2,128)(2,1)S(1)}, u32[]{:S(2)}, u32[]{:S(2)}) async-start(bf16[4,2,64]{2,1,0:T(2,128)(2,1)} %bitcast), calls=%async_computation | async-start | bytes 4096 | tf_op jit(solution)/shard_map/all_to_all | solution.py:279
  22.1 0.1 add_bitcast_fusion.freq
  22.2 0.7 %copy-done.9 = u32[32]{0:T(128)S(1)} copy-done((u32[32]{0:T(128)S(1)}, u32[32]{0:T(128)}, u32[]{:S(2)}) %copy-start.9) | copy-done | bytes 152
  22.9 0.6 dynamic-slice
  24.1 0.1 dynamic_slice.6
  24.2 0.7 copy-done.8
  24.8 0.2 dynamic-update-slice
  25.0 8.8 %all-reduce.2 = s32[64]{0:T(128)S(1)} all-reduce(s32[64]{0:T(128)S(1)} %dynamic-update-slice), channel_id=1, replica_groups=mesh['grp'=2,'ch'=4,'tm'=2,'sub'=2] {'ch'}, use_global_device_ids=true, to_apply=%add.2 | all-reduce | flops 64 | bytes 512
  33.8 0.0 all-to-all-done
  33.8 0.1 reshape.41
  33.9 0.1 squeeze.8
  34.0 0.1 squeeze.9
  34.1 0.4 fusion.17
  34.5 0.4 fusion.21
  34.9 0.4 fusion.2
  35.3 0.4 fusion.3
  35.7 0.4 fusion.19
  36.2 0.4 fusion.15
  36.6 0.4 fusion.1
  37.0 0.4 fusion
  37.5 0.1 fusion.33
  37.6 0.7 %reshape.49 = bf16[2,4,96]{2,0,1:T(2,128)(2,1)} reshape(bf16[2,4,2,48]{3,2,0,1:T(2,128)(2,1)S(1)} %copy.34) | data formatting | bytes 3072 | tf_op jit(solution)/shard_map/all_to_all | solution.py:296
  38.3 3.2 %all-to-all-start.1 = ((bf16[2,4,96]{2,0,1:T(2,128)(2,1)}), bf16[2,4,96]{2,0,1:T(2,128)(2,1)S(1)}, u32[]{:S(2)}, u32[]{:S(2)}) async-start(bf16[2,4,96]{2,0,1:T(2,128)(2,1)} %reshape.49), calls=%async_computation.1 | async-start | bytes 4096 | tf_op jit(solution)/shard_map/all_to_all | solution.py:296
  41.5 0.1 convert_bitcast_fusion
  41.6 0.1 copy.32.pick
  41.7 0.1 copy.33.ws
  41.8 0.0 copy-start.2
  41.8 5.1 %all-to-all-done.1 = bf16[2,4,96]{2,0,1:T(2,128)(2,1)S(1)} async-done(((bf16[2,4,96]{2,0,1:T(2,128)(2,1)}), bf16[2,4,96]{2,0,1:T(2,128)(2,1)S(1)}, u32[]{:S(2)}, u32[]{:S(2)}) %all-to-all-start.1) | async-done | bytes 1568 | tf_op jit(solution)/shard_map/all_to_all | solution.py:296
  46.9 5.3 %all_gather.6 = bf16[32,96]{1,0:T(8,128)(2,1)S(1)} all-gather(bf16[8,96]{1,0:T(8,128)(2,1)S(1)} %bitcast.45), channel_id=1, replica_groups=mesh['grp'=2,'ch'=4,'tm'=2,'sub'=2] {'tm','sub'}, dimensions={0}, use_global_device_ids=true | all-gather | bytes 7680 | tf_op jit(solution)/shard_map/all_gather | solution.py:297
  52.3 0.1 reshape.42
  52.3 0.0 copy-start.3
  52.4 0.1 copy.31.pb
  52.4 0.0 copy-done.1
  52.5 0.0 copy-done.2
  52.5 0.6 copy-done.3
  53.0 0.1 copy-done.4
  53.1 12.1 %shard_map.112 = (bf16[32,256]{1,0:T(8,128)(2,1)}, f32[16,128]{1,0:T(8,128)}, f32[32,256]{1,0:T(8,128)}) custom-call(bf16[48,64]{1,0:T(8,128)(2,1)S(1)} %copy.31.pb, s32[1,64]{1,0:T(1,128)S(1)} %add_bitcast_fusion.freq, f32[24,1]{1,0:T(8,128)S(1)} %copy.32.pick, bf16[9,32]{1,0:T(8,128)(2,1)S(1)} %copy-done.3, bf16[9,32,32]{2,1,0:T(8,128)(2,1)S(1)} %copy-done.2, ...), custom_call_target="tpu_custom_call" | custom-call | tf_op jit(solution)/shard_map/pallas_call | solution.py:313
  (18 shorter events, 0.1 us)
Async XLA Ops:
  0.6 0.7 %copy-start = (bf16[32,256]{1,0:T(8,128)(2,1)S(1)}, bf16[32,256]{1,0:T(8,128)(2,1)}, u32[]{:S(2)}) copy-start(bf16[32,256]{1,0:T(8,128)(2,1)} %param.9) | copy-start | bytes 49156
  0.7 0.7 %copy-start.6 = (s32[32]{0:T(128)S(1)}, s32[32]{0:T(128)}, u32[]{:S(2)}) copy-start(s32[32]{0:T(128)} %param.10) | copy-start | bytes 388
  14.8 0.7 %copy-start.10 = (u32[32]{0:T(128)S(1)}, u32[32]{0:T(128)}, u32[]{:S(2)}) copy-start(u32[32]{0:T(128)} %constant.77) | copy-start | bytes 388
  17.2 16.6 %all-to-all-start = ((bf16[4,2,64]{2,1,0:T(2,128)(2,1)}), bf16[4,2,64]{2,1,0:T(2,128)(2,1)S(1)}, u32[]{:S(2)}, u32[]{:S(2)}) async-start(bf16[4,2,64]{2,1,0:T(2,128)(2,1)} %bitcast), calls=%async_computation | async-start | bytes 4096 | tf_op jit(solution)/shard_map/all_to_all | solution.py:279
  22.2 0.7 %copy-start.9 = (u32[32]{0:T(128)S(1)}, u32[32]{0:T(128)}, u32[]{:S(2)}) copy-start(u32[32]{0:T(128)} %constant.71) | copy-start | bytes 388
  23.4 0.7 %copy-start.7 = (s32[32]{0:T(128)S(1)}, s32[32]{0:T(128)}, u32[]{:S(2)}) copy-start(s32[32]{0:T(128)} %param.11) | copy-start | bytes 388
  24.2 0.7 %copy-start.8 = (s32[16]{0:T(128)S(1)}, s32[16]{0:T(128)}, u32[]{:S(2)}) copy-start(s32[16]{0:T(128)} %param.12) | copy-start | bytes 196
  37.0 4.6 %copy-start.5 = (bf16[4,64,32]{1,2,0:T(8,128)(2,1)S(1)}, bf16[4,64,32]{1,2,0:T(8,128)(2,1)}, u32[]{:S(2)}) copy-start(bf16[4,64,32]{1,2,0:T(8,128)(2,1)} %param.15) | copy-start | bytes 49156
  37.4 15.0 %copy-start.1 = (bf16[9,64,64]{2,1,0:T(8,128)(2,1)S(1)}, bf16[9,64,64]{2,1,0:T(8,128)(2,1)}, u32[]{:S(2)}) copy-start(bf16[9,64,64]{2,1,0:T(8,128)(2,1)} %w3.1) | copy-start | bytes 221188
  38.3 8.7 %all-to-all-start.1 = ((bf16[2,4,96]{2,0,1:T(2,128)(2,1)}), bf16[2,4,96]{2,0,1:T(2,128)(2,1)S(1)}, u32[]{:S(2)}, u32[]{:S(2)}) async-start(bf16[2,4,96]{2,0,1:T(2,128)(2,1)} %reshape.49), calls=%async_computation.1 | async-start | bytes 4096 | tf_op jit(solution)/shard_map/all_to_all | solution.py:296
  41.8 10.7 %copy-start.2 = (bf16[9,32,32]{2,1,0:T(8,128)(2,1)S(1)}, bf16[9,32,32]{2,1,0:T(8,128)(2,1)}, u32[]{:S(2)}) copy-start(bf16[9,32,32]{2,1,0:T(8,128)(2,1)} %w2.1) | copy-start | bytes 55300
  52.3 0.7 %copy-start.3 = (bf16[9,32]{1,0:T(8,128)(2,1)S(1)}, bf16[9,32]{1,0:T(8,128)(2,1)}, u32[]{:S(2)}) copy-start(bf16[9,32]{1,0:T(8,128)(2,1)} %w1.1) | copy-start | bytes 1732
  52.4 0.7 %copy-start.4 = (bf16[64]{0:T(256)(128)(2,1)S(1)}, bf16[64]{0:T(256)(128)(2,1)}, u32[]{:S(2)}) copy-start(bf16[64]{0:T(256)(128)(2,1)} %param.17) | copy-start | bytes 388

commit v2 on v1

--- a/solution.py
+++ b/solution.py
@@ -255,7 +255,126 @@
     )
 
 
-def wave_tables(total, channels_out=None):
+def exchange_kernel(samples, record, freq, pick, out, mine, landed, gath, sems_t, sems_c):
+    grp, ch, tm, sub = (lax.axis_index(name) for name in ("grp", "ch", "tm", "sub"))
+    groups = lax.axis_size("ch")
+    time_partners = [(tm, 1 - sub), (1 - tm, sub), (1 - tm, 1 - sub)]
+    targets = [(grp, ch, t, s) for t, s in time_partners]
+    targets += [(grp, lax.rem(ch + d, groups), tm, sub) for d in range(1, groups)]
+    barrier = pltpu.get_barrier_semaphore()
+    for target in targets:
+        pl.semaphore_signal(barrier, inc=1, device_id=target, device_id_type=pl.DeviceIdType.MESH)
+    chans, times = record.shape
+    freqs = freq.shape[1]
+    half = chans // 2
+    freq_row = jnp.concatenate([freq[...], freq[...]], axis=1)
+    high, low = split(table(freq_row, freqs, (tm * 2 + sub) * times, 1, times, samples))
+    part = mm(record[...], high) + mm(record[...], low)
+    mine[...] = jnp.concatenate([part[:half], part[half:]], axis=1)
+    pl.semaphore_wait(barrier, len(targets))
+    copies = []
+    for d in range(3):
+        copies.append(
+            pltpu.make_async_remote_copy(
+                src_ref=mine,
+                dst_ref=landed.at[d],
+                send_sem=sems_t.at[0, d],
+                recv_sem=sems_t.at[1, d],
+                device_id=targets[d],
+                device_id_type=pl.DeviceIdType.MESH,
+            )
+        )
+        copies[-1].start()
+    picks = jnp.broadcast_to(pick[...], (8, pick.shape[1])).astype(F32).T[:, :1]
+    coarse = jnp.floor(picks * 0.125)
+    side = jnp.concatenate([coarse, picks - 8.0 * coarse], axis=1)
+    side = jnp.concatenate([side, jnp.zeros((half, 2 * freqs - 2), F32)], axis=1)
+    side = jnp.concatenate([side, jnp.zeros_like(side)], axis=0)
+    for copy in copies:
+        copy.wait()
+    total = (mine[...] + landed[0]) + (landed[1] + landed[2])
+    spectrum = jnp.concatenate([total[:, : 2 * freqs], total[:, 2 * freqs :]], axis=0)
+    gath[ch] = jnp.concatenate([spectrum, side], axis=1).astype(BF16)
+    copies = []
+    for d in range(1, groups):
+        copies.append(
+            pltpu.make_async_remote_copy(
+                src_ref=gath.at[ch],
+                dst_ref=gath.at[ch],
+                send_sem=sems_c.at[0, d - 1],
+                recv_sem=sems_c.at[1, d - 1],
+                device_id=targets[2 + d],
+                device_id_type=pl.DeviceIdType.MESH,
+            )
+        )
+        copies[-1].start()
+    for copy in copies:
+        copy.wait()
+    out[...] = gath[...]
+
+
+def exchange(record, freq_bins, pick_index, samples):
+    groups = lax.axis_size("ch")
+    chans = record.shape[0]
+    lanes = 4 * freq_bins.shape[0]
+    vmem = pl.BlockSpec(memory_space=pltpu.VMEM)
+    return pl.pallas_call(
+        functools.partial(exchange_kernel, samples),
+        out_shape=jax.ShapeDtypeStruct((groups, chans, lanes), BF16),
+        in_specs=[vmem] * 3,
+        out_specs=vmem,
+        scratch_shapes=[
+            pltpu.VMEM((chans // 2, lanes), F32),
+            pltpu.VMEM((3, chans // 2, lanes), F32),
+            pltpu.VMEM((groups, chans, lanes), BF16),
+            pltpu.SemaphoreType.DMA((2, 3)),
+            pltpu.SemaphoreType.DMA((2, groups - 1)),
+        ],
+        compiler_params=pltpu.CompilerParams(collective_id=0, has_side_effects=True),
+    )(record, freq_bins[None], pick_index[None])
+
+
+def dft_table(first_row, rows, total):
+    at = first_row + lax.broadcasted_iota(jnp.int32, (rows, 2 * total), 0)
+    lane = lax.broadcasted_iota(jnp.int32, (rows, 2 * total), 1)
+    quarter = jnp.where(lane >= total, 3 * total // 4, 0)
+    return split(cosine_turns((at * (lane & (total - 1)) + quarter) & (total - 1), total))
+
+
+def small_kernel(geo, samples, freqs, gath, freq, limit, w1, w2, ws, w3, wh, *rest):
+    me_ch, me_t = lax.axis_index("ch"), lax.axis_index("tm") * lax.axis_size("sub") + lax.axis_index("sub")
+    groups, chans, _ = gath.shape
+    total = groups * chans
+    both = 2 * freqs
+    spec = jnp.concatenate([gath[g].astype(F32) for g in range(groups)], axis=0)
+    re, im = spec[:, :freqs], spec[:, freqs:both]
+    stack = jnp.concatenate(
+        [jnp.concatenate([re, im], axis=1), jnp.concatenate([im, -re], axis=1)], axis=0
+    ).astype(BF16)
+    high, low = dft_table(0, total, total)
+    wave = mm(high, stack) + mm(low, stack)
+    index = lax.broadcasted_iota(jnp.int32, (total, both), 0)
+    limits = jnp.concatenate([limit[...], limit[...]], axis=1)
+    wave = jnp.where(jnp.minimum(index, total - index) <= limits, wave, 0.0)
+    re, im = wave[:, :freqs], wave[:, freqs:]
+    stack_h, stack_l = split(jnp.concatenate([wave, jnp.concatenate([-im, re], axis=1)], axis=0))
+    high, low = dft_table(me_ch * chans - 2 * HALO + total, chans + 4 * HALO, total)
+    pb = (mm(high, stack_h) + mm(low, stack_h) + mm(high, stack_l)) * (1.0 / total)
+    around = [jnp.maximum(me_ch - 1, 0), me_ch, jnp.minimum(me_ch + 1, groups - 1)]
+    rows = geo.rows
+    picks = []
+    for g, (first, last) in zip(around, ((rows - HALO, rows), (0, rows), (0, HALO))):
+        side = gath[g].astype(F32)[first:last]
+        picks.append(side[:, both : both + 1] * 8.0 + side[:, both + 1 : both + 2])
+    pick_col = jnp.concatenate(picks, axis=0)
+    freq_row = jnp.concatenate([freq[...], freq[...]], axis=1)
+    unet(
+        geo, samples, total // 2, pb.astype(BF16), freq_row, freqs, pick_col, me_ch, me_t,
+        (w1, w2, ws, w3, wh), rest[:3], rest[3:],
+    )
+
+
+def wave_tables(total):
     index = jnp.arange(total, dtype=jnp.int32)
     angle = (index[:, None] * index[None, :] % total).astype(F32) * (2.0 * math.pi / total)
     return jnp.cos(angle), jnp.sin(angle)
@@ -305,18 +424,25 @@
     total_chans = local_chans * chan_groups
     freqs = freq_bins.shape[0]
     geo = Geometry(local_chans // 2, local_times // 2)
-    pb = spectral_wide(record, freq_bins, wave_limit, geo, samples, total_chans)
-    freq_row = jnp.concatenate([freq_bins, freq_bins])[None]
-    picks = jnp.pad(lax.all_gather(pick_index, "ch", axis=0, tiled=True), (HALO, HALO))
-    picks = lax.dynamic_slice_in_dim(picks, lax.axis_index("ch") * geo.rows, geo.high)
     vmem = pl.BlockSpec(memory_space=pltpu.VMEM)
-    return pl.pallas_call(
-        functools.partial(step_kernel, geo, samples, total_chans // 2, freqs),
+    call = dict(
         out_shape=out_shapes(geo),
         in_specs=[vmem] * 8,
         out_specs=(vmem,) * 3,
         scratch_shapes=unet_scratch(geo, w2.shape[1], w3.shape[1]),
         compiler_params=pltpu.CompilerParams(vmem_limit_bytes=48 * 2**20),
+    )
+    if lax.axis_size("tm") == 2 and lax.axis_size("sub") == 2 and freqs == 32 and total_chans <= 256:
+        gath = exchange(record, freq_bins, pick_index, samples)
+        return pl.pallas_call(functools.partial(small_kernel, geo, samples, freqs), **call)(
+            gath, freq_bins[None], wave_limit[None], w1, w2, ws, w3, wh[None]
+        )
+    pb = spectral_wide(record, freq_bins, wave_limit, geo, samples, total_chans)
+    freq_row = jnp.concatenate([freq_bins, freq_bins])[None]
+    picks = jnp.pad(lax.all_gather(pick_index, "ch", axis=0, tiled=True), (HALO, HALO))
+    picks = lax.dynamic_slice_in_dim(picks, lax.axis_index("ch") * geo.rows, geo.high)
+    return pl.pallas_call(
+        functools.partial(step_kernel, geo, samples, total_chans // 2, freqs), **call
     )(pb, freq_row, picks.astype(F32)[:, None], w1, w2, ws, w3, wh[None])
 
 

time: 65.7 us -> 28.1 us (0.43)
  blocking collectives: 26.8 us -> 0 us
  Pallas kernels: 12.1 us -> 24.6 us
  starting transfers between devices: 8.09 us -> 0 us
  waiting for transfers between devices: 5.14 us -> 0 us
  local copies, waits for them, and re-layouts: 6.72 us -> 2.54 us
  matrix products: 3.99 us -> 0 us
  between operations: 2.11 us -> 0.73 us
    unnamed x2 -> x0, blocking collectives: 21.4 us -> none
    pallas_call x1 -> x2, Pallas kernels: 12.1 us -> 24.6 us  [the longest x1 12.5 us: local(): pl.pallas_call(functools.partial(small_kernel, geo, samples, freqs), **call)]
    all_to_all x2 -> x0, starting transfers between devices: 8.09 us -> none  [the longest x1 4.87 us: spectral_wide(): lax.all_to_all(summed.astype(BF16), 'ch', split_axis=0, concat_axis=1, ti...]
    all_gather x1 -> x0, blocking collectives: 5.33 us -> none  [spectral_wide(): values = lax.all_gather(returned, ('tm', 'sub'), axis=0, tiled=True)]
    all_to_all x2 -> x0, waiting for transfers between devices: 5.14 us -> none  [the longest x1 5.14 us: spectral_wide(): lax.all_to_all(outgoing, 'ch', split_axis=1, concat_axis=0, tiled=True)]
    dot_general x10 -> x0, matrix products: 3.99 us -> none  [the longest x2 0.83 us: spectral_wide(): re = dot(arranged[0], cosine) + dot(arranged[1], sine)]
    unnamed x27 -> x15, local copies, waits for them, and re-layouts: 4.76 us -> 2.54 us
    all_to_all x3 -> x0, local copies, waits for them, and re-layouts: 0.67 us -> none  [the longest x2 0.67 us: spectral_wide(): lax.all_to_all(outgoing, 'ch', split_axis=1, concat_axis=0, tiled=True)]
  transfers between devices with their start and end apart: 2 -> 0, of which waited for: 1 -> 0; matrix products, arithmetic and copies ran while one was open for 2% -> 0% of each run, Pallas kernels for 0% -> 0%
where the time goes in v2:
time: 28.1 us; the launch traced here: 27.8 us
  Pallas kernels  24.6 us (88%)
  local copies, waits for them, and re-layouts  2.54 us (9%)
  between operations  0.73 us (3%)
    pallas_call x1, Pallas kernels, local(): pl.pallas_call(functools.partial(small_kernel, geo, samples, freqs), **call)  12.5 us
    pallas_call x1, Pallas kernels, exchange(): pl.pallas_call(functools.partial(exchange_kernel, samples), out_shape=jax...  12.1 us
    unnamed x15, local copies, waits for them, and re-layouts  2.54 us

profile of v2, /device:TPU:0, one launch (start us, length us, event | category | flops | bytes accessed | tf_op | source)
XLA Modules:
  0.0 27.8 jit_solution(7420056114581512887)
XLA Ops:
  0.6 0.0 copy-start
  0.6 12.1 %shard_map.112.gath = bf16[4,32,128]{2,1,0:T(8,128)(2,1)} custom-call(bf16[32,256]{1,0:T(8,128)(2,1)} %record.1, s32[1,32]{1,0:T(1,128)} %bitcast.4, s32[1,16]{1,0:T(1,128)} %bitcast.8), custom_call_target="tpu_custom_call" | custom-call | tf_op jit(solution)/shard_map/pallas_call | solution.py:321
  12.7 0.0 copy-start.3
  12.8 0.0 copy-start.4
  12.8 0.0 copy-start.5
  12.8 0.0 copy-start.6
  12.8 0.9 %copy.12.ws = bf16[4,64,32]{2,1,0:T(8,128)(2,1)S(1)} copy(bf16[4,64,32]{1,2,0:T(8,128)(2,1)} %param.15) | data formatting | bytes 32768 | tf_op args[6]
  13.7 0.0 copy-done
  13.7 0.0 copy-done.3
  13.7 0.0 copy-done.4
  13.7 0.0 copy-done.5
  13.7 0.0 copy-done.6
  13.7 0.0 copy-start.1
  13.7 0.7 %copy-done.1 = bf16[4,32,128]{2,1,0:T(8,128)(2,1)S(1)} copy-done((bf16[4,32,128]{2,1,0:T(8,128)(2,1)S(1)}, bf16[4,32,128]{2,1,0:T(8,128)(2,1)}, u32[]{:S(2)}) %copy-start.1) | copy-done | bytes 32792
  14.5 0.0 copy-start.2
  14.5 0.9 %copy-done.2 = bf16[9,32,32]{2,1,0:T(8,128)(2,1)S(1)} copy-done((bf16[9,32,32]{2,1,0:T(8,128)(2,1)S(1)}, bf16[9,32,32]{2,1,0:T(8,128)(2,1)}, u32[]{:S(2)}) %copy-start.2) | copy-done | bytes 18456
  15.4 12.5 %shard_map.113 = (bf16[32,256]{1,0:T(8,128)(2,1)}, f32[16,128]{1,0:T(8,128)}, f32[32,256]{1,0:T(8,128)}) custom-call(bf16[4,32,128]{2,1,0:T(8,128)(2,1)S(1)} %copy-done.1, s32[1,32]{1,0:T(1,128)S(1)} %bitcast.5, s32[1,32]{1,0:T(1,128)S(1)} %bitcast.6, bf16[9,32]{1,0:T(8,128)(2,1)S(1)} %copy-done.3, bf16[9,32,32]{2,1,0:T(8,128)(2,1)S(1)} %copy-done.2, ...), custom_call_target="tpu_custom_call" | custom-call | tf_op jit(solution)/shard_map/pallas_call | solution.py:437
Async XLA Ops:
  0.6 13.0 %copy-start = (bf16[9,64,64]{2,1,0:T(8,128)(2,1)S(1)}, bf16[9,64,64]{2,1,0:T(8,128)(2,1)}, u32[]{:S(2)}) copy-start(bf16[9,64,64]{2,1,0:T(8,128)(2,1)} %w3.1) | copy-start | bytes 221188
  12.7 0.9 %copy-start.3 = (bf16[9,32]{1,0:T(8,128)(2,1)S(1)}, bf16[9,32]{1,0:T(8,128)(2,1)}, u32[]{:S(2)}) copy-start(bf16[9,32]{1,0:T(8,128)(2,1)} %w1.1) | copy-start | bytes 1732
  12.8 0.9 %copy-start.4 = (s32[32]{0:T(128)S(1)}, s32[32]{0:T(128)}, u32[]{:S(2)}) copy-start(s32[32]{0:T(128)} %param.10) | copy-start | bytes 388
  12.8 0.9 %copy-start.5 = (s32[32]{0:T(128)S(1)}, s32[32]{0:T(128)}, u32[]{:S(2)}) copy-start(s32[32]{0:T(128)} %param.11) | copy-start | bytes 388
  12.8 0.9 %copy-start.6 = (bf16[64]{0:T(256)(128)(2,1)S(1)}, bf16[64]{0:T(256)(128)(2,1)}, u32[]{:S(2)}) copy-start(bf16[64]{0:T(256)(128)(2,1)} %param.17) | copy-start | bytes 388
  13.7 0.8 %copy-start.1 = (bf16[4,32,128]{2,1,0:T(8,128)(2,1)S(1)}, bf16[4,32,128]{2,1,0:T(8,128)(2,1)}, u32[]{:S(2)}) copy-start(bf16[4,32,128]{2,1,0:T(8,128)(2,1)} %shard_map.112.gath) | copy-start | bytes 98308
  14.5 0.9 %copy-start.2 = (bf16[9,32,32]{2,1,0:T(8,128)(2,1)S(1)}, bf16[9,32,32]{2,1,0:T(8,128)(2,1)}, u32[]{:S(2)}) copy-start(bf16[9,32,32]{2,1,0:T(8,128)(2,1)} %w2.1) | copy-start | bytes 55300

commit v3 on v2

--- a/solution.py
+++ b/solution.py
@@ -13,6 +13,7 @@
 MARGIN = 256
 F32 = jnp.float32
 BF16 = jnp.bfloat16
+PHASES = [(a, b) for a in (0, 1) for b in (0, 1)]
 SHIFTS = [(sy, sx) for sy in (-1, 0, 1) for sx in (-1, 0, 1)]
 PATCH = [(y, x) for y in (-1, 0, 1, 2) for x in (-1, 0, 1, 2)]
 
@@ -61,31 +62,60 @@
         self.size = self.high * self.pitch
         self.padded = -(-self.size // 256) * 256
         self.width = self.padded + 2 * MARGIN
-        count = 2
-        tiles = self.padded // 128
-        self.chunks = []
-        at = 0
-        for i in range(count):
-            end = tiles * (i + 1) // count
-            self.chunks.append((at * 128, (end - at) * 128))
-            at = end
+
+    def chunks(self, margin, count=2):
+        first = margin * self.pitch // 128
+        last = -(-(self.high - margin) * self.pitch // 128)
+        last += (last - first) % 2
+        cuts = [first + (last - first) * i // count for i in range(count + 1)]
+        return [(lo * 128, (hi - lo) * 128) for lo, hi in zip(cuts, cuts[1:])]
 
     def offset(self, sy, sx):
         return sy * self.pitch + sx
 
 
-def unet(geo, samples, total_rows, pb, freq_row, freqs, pick_col, me_ch, me_t, refs, outs, scr):
-    w1_ref, w2_ref, ws_ref, w3_ref, wh_ref = refs
+def conv_weights(w2_in, ws_in, w3_in):
+    w2 = [w2_in[k].astype(F32) for k in range(9)]
+    zero = jnp.zeros_like(w2[0])
+
+    def tap(y, x, a, b, sign):
+        ky, kx = sign * (y - a) + 1, sign * (x - b) + 1
+        return w2[3 * ky + kx] if 0 <= ky < 3 and 0 <= kx < 3 else zero
+
+    w2_f = jnp.concatenate(
+        [jnp.concatenate([tap(y, x, a, b, 1) for y, x in PATCH], axis=1) for a, b in PHASES], axis=0
+    ).astype(BF16)
+    w2_b = jnp.concatenate(
+        [jnp.concatenate([tap(y, x, a, b, -1) for a, b in PHASES], axis=1) for y, x in PATCH], axis=0
+    ).T.astype(BF16)
+    ws_f32 = jnp.concatenate([ws_in[k].astype(F32) for k in range(4)], axis=0)
+    ws_f, ws_b = ws_f32.T.astype(BF16), ws_f32.astype(BF16)
+    w3 = [w3_in[k].astype(F32) for k in range(9)]
+    w3_f = jnp.concatenate(w3, axis=1).astype(BF16)
+    w3_b = jnp.concatenate(w3, axis=0).T.astype(BF16)
+    return w2_f, w2_b, ws_f, ws_b, w3_f, w3_b
+
+
+def unet_tables(freq_row, freqs, me_t, geo, samples):
+    first = me_t * 2 * geo.cols
+    found = split(table(freq_row, freqs, first, 1, 2 * geo.cols, samples))
+    for b in range(2):
+        found += split(table(freq_row, freqs, first - 2 * HALO + b, 2, geo.pitch, samples))
+    return found
+
+
+def unet(geo, samples, total_rows, pb, tables, pick_col, me_ch, me_t, w1_ref, wh_ref, convs, outs, scr):
     filt_o, logit_o, grad_o = outs
     x0, mask_s, targ_s, act1, sl1, sl2, act_s, sls, dl3, dl2, zs, log_s, grad_s, un = scr
     rows, cols, pitch = geo.rows, geo.cols, geo.pitch
     total_cols = samples // 2
     scale = 2.0 / samples
-    f1 = w2_ref.shape[1]
-    for ref in (x0, act1, act_s, dl3, dl2, zs):
-        n = ref.shape[0]
-        ref[:, :MARGIN] = jnp.zeros((n, MARGIN), ref.dtype)
-        ref[:, MARGIN + geo.padded :] = jnp.zeros((n, MARGIN), ref.dtype)
+    f1 = w1_ref.shape[1]
+    for ref, margin in ((x0, 0), (act1, 0), (act_s, 1), (dl3, 2), (dl2, 3), (zs, 3)):
+        spans = geo.chunks(margin)
+        lead, last = MARGIN + spans[0][0], MARGIN + sum(spans[-1])
+        ref[:, :lead] = jnp.zeros((ref.shape[0], lead), ref.dtype)
+        ref[:, last:] = jnp.zeros((ref.shape[0], geo.width - last), ref.dtype)
     place = lax.broadcasted_iota(jnp.int32, (8, geo.padded), 1).astype(F32)[:1]
     row = jnp.floor((place + 0.5) * (1.0 / pitch))
     col = place - row * pitch
@@ -98,25 +128,7 @@
     pick = jnp.sum(jnp.where(rid == row, pick_col, 0.0), axis=0, keepdims=True)
     offs = (2.0 * gcol - pick) * (1.0 / SIGMA)
     targ_s[...] = jnp.broadcast_to(jnp.exp(-0.5 * offs * offs), targ_s.shape)
-    w2 = [w2_ref[k].astype(F32) for k in range(9)]
-    zero = jnp.zeros_like(w2[0])
-
-    def tap(y, x, a, b, sign):
-        ky, kx = sign * (y - a) + 1, sign * (x - b) + 1
-        return w2[3 * ky + kx] if 0 <= ky < 3 and 0 <= kx < 3 else zero
-
-    phases = [(a, b) for a in (0, 1) for b in (0, 1)]
-    w2_f = jnp.concatenate(
-        [jnp.concatenate([tap(y, x, a, b, 1) for y, x in PATCH], axis=1) for a, b in phases], axis=0
-    ).astype(BF16)
-    w2_b = jnp.concatenate(
-        [jnp.concatenate([tap(y, x, a, b, -1) for a, b in phases], axis=1) for y, x in PATCH], axis=0
-    ).T.astype(BF16)
-    ws_f32 = jnp.concatenate([ws_ref[k].astype(F32) for k in range(4)], axis=1)
-    ws_f, ws_b = ws_f32.astype(BF16), ws_f32.T.astype(BF16)
-    w3 = [w3_ref[k].astype(F32) for k in range(9)]
-    w3_f = jnp.concatenate(w3, axis=1).astype(BF16)
-    w3_b = jnp.concatenate(w3, axis=0).T.astype(BF16)
+    w2_f, w2_b, ws_f, ws_b, w3_f, w3_b = (value[...] for value in convs)
     head = jnp.broadcast_to(wh_ref[...].astype(F32), (8, wh_ref.shape[1]))
     head_col = head.T[:, :1]
     head_row = head.astype(BF16)
@@ -124,10 +136,10 @@
     tapi = lax.broadcasted_iota(jnp.int32, (72, 9), 1)
     w1 = w1_ref[...]
     parts = []
-    for a, b in phases:
+    for a, b in PHASES:
         sel = jnp.zeros((72, 9), F32)
         for s, (sy, sx) in enumerate(SHIFTS):
-            for p, (py, px) in enumerate(phases):
+            for p, (py, px) in enumerate(PHASES):
                 ky, kx = 2 * sy + py - a + 1, 2 * sx + px - b + 1
                 if 0 <= ky < 3 and 0 <= kx < 3:
                     sel = jnp.where((srow == 8 * s + p) & (tapi == 3 * ky + kx), 1.0, sel)
@@ -135,14 +147,12 @@
     w1_b32 = jnp.concatenate(parts, axis=1)
     w1_f, w1_b = w1_b32.T.astype(BF16), w1_b32.astype(BF16)
 
-    nat_h, nat_l = split(table(freq_row, freqs, me_t * 2 * cols, 1, 2 * cols, samples))
+    nat_h, nat_l = tables[0][...], tables[1][...]
     nat = (mm_nt(pb, nat_h) + mm_nt(pb, nat_l)) * scale
     filt_o[...] = nat[2 * HALO : 2 * HALO + 2 * rows].astype(BF16)
     x0[...] = jnp.zeros_like(x0)
     for b in range(2):
-        t_h, t_l = split(
-            table(freq_row, freqs, me_t * 2 * cols - 2 * HALO + b, 2, geo.pitch, samples)
-        )
+        t_h, t_l = tables[2 + 2 * b][...], tables[3 + 2 * b][...]
         un[:, :pitch] = (mm_nt(pb, t_h) + mm_nt(pb, t_l)) * scale
         for r in range(geo.high):
             at = MARGIN + r * pitch
@@ -150,7 +160,7 @@
                 x0[2 * a + b : 2 * a + b + 1, at : at + pitch] = un[2 * r + a : 2 * r + a + 1, :pitch]
     x0[:, MARGIN : MARGIN + geo.padded] = x0[:, MARGIN : MARGIN + geo.padded] * mask_s[...]
 
-    for at, n in geo.chunks:
+    for at, n in geo.chunks(0):
         patches = jnp.concatenate(
             [x0[:, MARGIN + at + geo.offset(*s) : MARGIN + at + geo.offset(*s) + n] for s in SHIFTS], axis=0
         ).astype(BF16)
@@ -173,29 +183,29 @@
             blocks.append(ref[:, start : start + n])
         return jnp.concatenate(blocks, axis=0)
 
-    for at, n in geo.chunks:
+    for at, n in geo.chunks(1):
         y, slope = silu_parts(mm(w2_f, fine_patches(act1, at, n)))
         sl2[:, at : at + n] = slope
         y, slope = silu_parts(mm(ws_f, y.astype(BF16)))
         act_s[:, MARGIN + at : MARGIN + at + n] = (y * mask_s[:1, at : at + n]).astype(BF16)
         sls[:, at : at + n] = slope
-    for at, n in geo.chunks:
+    for at, n in geo.chunks(2):
         y, slope = silu_parts(mm(w3_f, coarse_patches(act_s, at, n, 1)))
         logits = mm(head_row, y.astype(BF16))
         log_s[:, at : at + n] = logits
         out = (0.5 * jnp.tanh(0.5 * logits) + 0.5 - targ_s[:, at : at + n]) * mask_s[:, at : at + n]
         dl3[:, MARGIN + at : MARGIN + at + n] = (head_col * out[:1] * slope).astype(BF16)
-    for at, n in geo.chunks:
+    for at, n in geo.chunks(3):
         back = mm(w3_b, coarse_patches(dl3, at, n, -1))
         back = mm(ws_b, (back * sls[:, at : at + n]).astype(BF16))
         dl2[:, MARGIN + at : MARGIN + at + n] = (
             back * sl2[:, at : at + n] * mask_s[:1, at : at + n]
         ).astype(BF16)
-    for at, n in geo.chunks:
+    for at, n in geo.chunks(3):
         back = mm(w2_b, fine_patches(dl2, at, n))
         delta = (back * sl1[:, at : at + n] * mask_s[:1, at : at + n]).astype(BF16)
         zs[:, MARGIN + at : MARGIN + at + n] = mm(w1_b, delta)
-    for at, n in geo.chunks:
+    for at, n in geo.chunks(4):
         total = None
         for s, shift in enumerate(SHIFTS):
             start = MARGIN + at - geo.offset(*shift)
@@ -249,13 +259,16 @@
 
 def step_kernel(geo, samples, total_rows, freqs, pb, freq, pick, w1, w2, ws, w3, wh, *rest):
     me_ch, me_t = lax.axis_index("ch"), lax.axis_index("tm") * lax.axis_size("sub") + lax.axis_index("sub")
+    tables = unet_tables(freq[...], freqs, me_t, geo, samples)
     unet(
-        geo, samples, total_rows, pb[...], freq[...], freqs, pick[...], me_ch, me_t,
-        (w1, w2, ws, w3, wh), rest[:3], rest[3:],
-    )
-
-
-def exchange_kernel(samples, record, freq, pick, out, mine, landed, gath, sems_t, sems_c):
+        geo, samples, total_rows, pb[...], tables, pick[...], me_ch, me_t, w1, wh,
+        conv_weights(w2, ws, w3), rest[:3], rest[3:],
+    )
+
+
+def exchange_kernel(geo, samples, *refs):
+    hbm, outs, held = refs[:6], refs[6:23], refs[23:29]
+    mine, landed, gath, sems_t, sems_c, sems_in = refs[29:]
     grp, ch, tm, sub = (lax.axis_index(name) for name in ("grp", "ch", "tm", "sub"))
     groups = lax.axis_size("ch")
     time_partners = [(tm, 1 - sub), (1 - tm, sub), (1 - tm, 1 - sub)]
@@ -264,11 +277,18 @@
     barrier = pltpu.get_barrier_semaphore()
     for target in targets:
         pl.semaphore_signal(barrier, inc=1, device_id=target, device_id_type=pl.DeviceIdType.MESH)
+    loads = [pltpu.make_async_copy(a, b, sems_in.at[i]) for i, (a, b) in enumerate(zip(hbm, held))]
+    for load in loads:
+        load.start()
+    record, freq, pick, w2, ws, w3 = held
     chans, times = record.shape
     freqs = freq.shape[1]
     half = chans // 2
+    for load in loads[:3]:
+        load.wait()
     freq_row = jnp.concatenate([freq[...], freq[...]], axis=1)
-    high, low = split(table(freq_row, freqs, (tm * 2 + sub) * times, 1, times, samples))
+    first = (tm * 2 + sub) * times
+    high, low = split(table(freq_row, freqs, first, 1, times, samples))
     part = mm(record[...], high) + mm(record[...], low)
     mine[...] = jnp.concatenate([part[:half], part[half:]], axis=1)
     pl.semaphore_wait(barrier, len(targets))
@@ -290,6 +310,10 @@
     side = jnp.concatenate([coarse, picks - 8.0 * coarse], axis=1)
     side = jnp.concatenate([side, jnp.zeros((half, 2 * freqs - 2), F32)], axis=1)
     side = jnp.concatenate([side, jnp.zeros_like(side)], axis=0)
+    for load in loads[3:]:
+        load.wait()
+    for ref, value in zip(outs[1:7], conv_weights(w2, ws, w3)):
+        ref[...] = value
     for copy in copies:
         copy.wait()
     total = (mine[...] + landed[0]) + (landed[1] + landed[2])
@@ -308,30 +332,50 @@
             )
         )
         copies[-1].start()
+    outs[7][...], outs[8][...] = high, low
+    for b in range(2):
+        extended = split(table(freq_row, freqs, first - 2 * HALO + b, 2, geo.pitch, samples))
+        outs[9 + 2 * b][...], outs[10 + 2 * b][...] = extended
+    total_chans = groups * chans
+    outs[13][...], outs[14][...] = dft_table(0, total_chans, total_chans)
+    outs[15][...], outs[16][...] = dft_table(
+        ch * chans - 2 * HALO + total_chans, chans + 4 * HALO, total_chans
+    )
     for copy in copies:
         copy.wait()
-    out[...] = gath[...]
-
-
-def exchange(record, freq_bins, pick_index, samples):
+    outs[0][...] = gath[...]
+
+
+def exchange(geo, record, freq_bins, pick_index, w2, ws, w3, samples):
     groups = lax.axis_size("ch")
     chans = record.shape[0]
-    lanes = 4 * freq_bins.shape[0]
+    freqs = freq_bins.shape[0]
+    lanes = 4 * freqs
+    f1, f2 = w2.shape[1], w3.shape[1]
+    total = groups * chans
+    args = (record, freq_bins[None], pick_index[None], w2, ws, w3)
+    shapes = [(groups, chans, lanes), (4 * f1, 16 * f1), (4 * f1, 16 * f1), (f2, 4 * f1), (4 * f1, f2)]
+    shapes += [(f2, 9 * f2)] * 2 + [(2 * geo.cols, 2 * freqs)] * 2 + [(geo.pitch, 2 * freqs)] * 4
+    shapes += [(total, 2 * total)] * 2 + [(chans + 4 * HALO, 2 * total)] * 2
     vmem = pl.BlockSpec(memory_space=pltpu.VMEM)
     return pl.pallas_call(
-        functools.partial(exchange_kernel, samples),
-        out_shape=jax.ShapeDtypeStruct((groups, chans, lanes), BF16),
-        in_specs=[vmem] * 3,
-        out_specs=vmem,
-        scratch_shapes=[
+        functools.partial(exchange_kernel, geo, samples),
+        out_shape=tuple(pltpu.VMEM(shape, BF16) for shape in shapes),
+        in_specs=[pl.BlockSpec(memory_space=pltpu.HBM)] * len(args),
+        out_specs=(vmem,) * len(shapes),
+        scratch_shapes=[pltpu.VMEM(arg.shape, arg.dtype) for arg in args]
+        + [
             pltpu.VMEM((chans // 2, lanes), F32),
             pltpu.VMEM((3, chans // 2, lanes), F32),
             pltpu.VMEM((groups, chans, lanes), BF16),
             pltpu.SemaphoreType.DMA((2, 3)),
             pltpu.SemaphoreType.DMA((2, groups - 1)),
+            pltpu.SemaphoreType.DMA((len(args),)),
         ],
-        compiler_params=pltpu.CompilerParams(collective_id=0, has_side_effects=True),
-    )(record, freq_bins[None], pick_index[None])
+        compiler_params=pltpu.CompilerParams(
+            collective_id=0, has_side_effects=True
+        ),
+    )(*args)
 
 
 def dft_table(first_row, rows, total):
@@ -341,7 +385,8 @@
     return split(cosine_turns((at * (lane & (total - 1)) + quarter) & (total - 1), total))
 
 
-def small_kernel(geo, samples, freqs, gath, freq, limit, w1, w2, ws, w3, wh, *rest):
+def small_kernel(geo, samples, freqs, limit, w1, wh, gath, *rest):
+    convs, tables, dfts, rest = rest[:6], rest[6:12], rest[12:16], rest[16:]
     me_ch, me_t = lax.axis_index("ch"), lax.axis_index("tm") * lax.axis_size("sub") + lax.axis_index("sub")
     groups, chans, _ = gath.shape
     total = groups * chans
@@ -351,14 +396,14 @@
     stack = jnp.concatenate(
         [jnp.concatenate([re, im], axis=1), jnp.concatenate([im, -re], axis=1)], axis=0
     ).astype(BF16)
-    high, low = dft_table(0, total, total)
+    high, low = dfts[0][...], dfts[1][...]
     wave = mm(high, stack) + mm(low, stack)
     index = lax.broadcasted_iota(jnp.int32, (total, both), 0)
     limits = jnp.concatenate([limit[...], limit[...]], axis=1)
     wave = jnp.where(jnp.minimum(index, total - index) <= limits, wave, 0.0)
     re, im = wave[:, :freqs], wave[:, freqs:]
     stack_h, stack_l = split(jnp.concatenate([wave, jnp.concatenate([-im, re], axis=1)], axis=0))
-    high, low = dft_table(me_ch * chans - 2 * HALO + total, chans + 4 * HALO, total)
+    high, low = dfts[2][...], dfts[3][...]
     pb = (mm(high, stack_h) + mm(low, stack_h) + mm(high, stack_l)) * (1.0 / total)
     around = [jnp.maximum(me_ch - 1, 0), me_ch, jnp.minimum(me_ch + 1, groups - 1)]
     rows = geo.rows
@@ -367,10 +412,9 @@
         side = gath[g].astype(F32)[first:last]
         picks.append(side[:, both : both + 1] * 8.0 + side[:, both + 1 : both + 2])
     pick_col = jnp.concatenate(picks, axis=0)
-    freq_row = jnp.concatenate([freq[...], freq[...]], axis=1)
     unet(
-        geo, samples, total // 2, pb.astype(BF16), freq_row, freqs, pick_col, me_ch, me_t,
-        (w1, w2, ws, w3, wh), rest[:3], rest[3:],
+        geo, samples, total // 2, pb.astype(BF16), tables, pick_col, me_ch, me_t, w1, wh,
+        convs, rest[:3], rest[3:],
     )
 
 
@@ -427,23 +471,27 @@
     vmem = pl.BlockSpec(memory_space=pltpu.VMEM)
     call = dict(
         out_shape=out_shapes(geo),
-        in_specs=[vmem] * 8,
         out_specs=(vmem,) * 3,
         scratch_shapes=unet_scratch(geo, w2.shape[1], w3.shape[1]),
         compiler_params=pltpu.CompilerParams(vmem_limit_bytes=48 * 2**20),
     )
     if lax.axis_size("tm") == 2 and lax.axis_size("sub") == 2 and freqs == 32 and total_chans <= 256:
-        gath = exchange(record, freq_bins, pick_index, samples)
-        return pl.pallas_call(functools.partial(small_kernel, geo, samples, freqs), **call)(
-            gath, freq_bins[None], wave_limit[None], w1, w2, ws, w3, wh[None]
+        ready = exchange(
+            geo, record, freq_bins, pick_index, w2, jnp.swapaxes(ws, 1, 2), w3, samples
         )
+        args = (wave_limit[None], w1, wh[None], *ready)
+        return pl.pallas_call(
+            functools.partial(small_kernel, geo, samples, freqs), in_specs=[vmem] * len(args), **call
+        )(*args)
     pb = spectral_wide(record, freq_bins, wave_limit, geo, samples, total_chans)
     freq_row = jnp.concatenate([freq_bins, freq_bins])[None]
     picks = jnp.pad(lax.all_gather(pick_index, "ch", axis=0, tiled=True), (HALO, HALO))
     picks = lax.dynamic_slice_in_dim(picks, lax.axis_index("ch") * geo.rows, geo.high)
     return pl.pallas_call(
-        functools.partial(step_kernel, geo, samples, total_chans // 2, freqs), **call
-    )(pb, freq_row, picks.astype(F32)[:, None], w1, w2, ws, w3, wh[None])
+        functools.partial(step_kernel, geo, samples, total_chans // 2, freqs),
+        in_specs=[vmem] * 8,
+        **call,
+    )(pb, freq_row, picks.astype(F32)[:, None], w1, w2, jnp.swapaxes(ws, 1, 2), w3, wh[None])
 
 
 def solution(mesh):

time: 28.1 us -> 23.6 us (0.84)
  Pallas kernels: 24.6 us -> 22 us
  local copies, waits for them, and re-layouts: 2.54 us -> 0.67 us
    pallas_call x2, Pallas kernels: 24.6 us -> 22 us  [the longest x1 11.2 us: exchange(): pl.pallas_call(functools.partial(exchange_kernel, geo, samples), out_shap...]
    unnamed x15 -> x6, local copies, waits for them, and re-layouts: 2.54 us -> 0.67 us
where the time goes in v3:
time: 23.6 us; the launch traced here: 23.3 us
  Pallas kernels  22 us (93%)
  local copies, waits for them, and re-layouts  0.67 us (3%)
  between operations  0.67 us (3%)
    pallas_call x1, Pallas kernels, exchange(): pl.pallas_call(functools.partial(exchange_kernel, geo, samples), out_shap...  11.2 us
    pallas_call x1, Pallas kernels, local(): pl.pallas_call(functools.partial(small_kernel, geo, samples, freqs), in_s...  10.7 us
    unnamed x6, local copies, waits for them, and re-layouts  0.67 us

profile of v3, /device:TPU:0, one launch (start us, length us, event | category | flops | bytes accessed | tf_op | source)
XLA Modules:
  0.0 23.3 jit_solution(4066403602176755356)
XLA Ops:
  0.6 11.2 %shard_map.112 = (bf16[4,32,128]{2,1,0:T(8,128)(2,1)S(1)}, bf16[128,512]{1,0:T(8,128)(2,1)S(1)}, bf16[128,512]{1,0:T(8,128)(2,1)S(1)}, bf16[64,128]{1,0:T(8,128)...) custom-call(bf16[32,256]{1,0:T(8,128)(2,1)} %refs_0_.1, ...), custom_call_target="tpu_custom_call" | custom-call | tf_op jit(solution)/shard_map/pallas_call | solution.py:361
  11.9 0.0 copy-start
  11.9 0.0 copy-start.1
  11.9 0.0 copy-start.2
  11.9 0.7 %copy-done = bf16[9,32]{1,0:T(8,128)(2,1)S(1)} copy-done((bf16[9,32]{1,0:T(8,128)(2,1)S(1)}, bf16[9,32]{1,0:T(8,128)(2,1)}, u32[]{:S(2)}) %copy-start) | copy-done | bytes 600
  12.6 0.0 copy-done.1
  12.6 0.0 copy-done.2
  12.6 10.7 %shard_map.113 = (bf16[32,256]{1,0:T(8,128)(2,1)}, f32[16,128]{1,0:T(8,128)}, f32[32,256]{1,0:T(8,128)}) custom-call(s32[1,32]{1,0:T(1,128)S(1)} %bitcast.5, bf16[9,32]{1,0:T(8,128)(2,1)S(1)} %copy-done, bf16[1,64]{1,0:T(2,128)(2,1)S(1)} %bitcast.6, bf16[4,32,128]{2,1,0:T(8,128)(2,1)S(1)} %get-tuple-element.20.gath, ...), custom_call_target="tpu_custom_call" | custom-call | tf_op jit(solution)/shard_map/pallas_call | solution.py:483
Async XLA Ops:
  11.9 0.7 %copy-start = (bf16[9,32]{1,0:T(8,128)(2,1)S(1)}, bf16[9,32]{1,0:T(8,128)(2,1)}, u32[]{:S(2)}) copy-start(bf16[9,32]{1,0:T(8,128)(2,1)} %w1.1) | copy-start | bytes 1732
  11.9 0.7 %copy-start.1 = (s32[32]{0:T(128)S(1)}, s32[32]{0:T(128)}, u32[]{:S(2)}) copy-start(s32[32]{0:T(128)} %param.11) | copy-start | bytes 388
  11.9 0.7 %copy-start.2 = (bf16[64]{0:T(256)(128)(2,1)S(1)}, bf16[64]{0:T(256)(128)(2,1)}, u32[]{:S(2)}) copy-start(bf16[64]{0:T(256)(128)(2,1)} %param.17) | copy-start | bytes 388
